TPU v7x, 512 devices: a whole 4x4x16 slice. The times are simulated.
512 devices in a mesh: ctx: 64 (over x_hi, z, core), grp: 8 (over x_lo, y).
Axes of the slice: x: 4 (x_hi: 2, x_lo: 2; x = x_hi * 2 + x_lo), y: 4, z: 16, core: 2. Of those that a mesh axis runs over, the one named last changes fastest.
Arguments:
- query_states: bfloat16 [8, 8192, 2048], P('grp', 'ctx'), may hold values from -2 to 2
- key_states: bfloat16 [8, 8192, 512], P('grp', 'ctx'), may hold values from -2 to 2
- value_states: bfloat16 [8, 8192, 512], P('grp', 'ctx'), may hold values from -6 to 6
- lengths: int32 [8], P('grp'), may hold values from 2048 to 8192, as said below
- queue_keys: bfloat16 [131072, 2048], P(('ctx', 'grp')), may hold values from -0.11481983 to 0.11481983
- write_pos: int32 [8], replicated, may hold values from 0 to 131071, as said below
- teacher: float32 [8, 131072], P(None, ('ctx', 'grp')), may hold values from -12 to 12
Outputs:
- loss_value: float32 [], replicated
- embedding: float32 [8, 2048], P('grp')
- grad_query: bfloat16 [8, 8192, 2048], P('grp', 'ctx')
- grad_key: bfloat16 [8, 8192, 512], P('grp', 'ctx')
- grad_value: bfloat16 [8, 8192, 512], P('grp', 'ctx')
Inputs may be any that keep to these rules, and one draw needn't show every extreme that they name: `lengths`: some document is full. `write_pos`: distinct entries.
All inputs are finite; a program needn't handle non-finite values.
Results may differ from a plain program's by a relative error of at most 0.0079.
Values may be sent and summed in bfloat16 or wider, within the bound.
A program may use at most 64 MiB of HBM per device.

v0:
```python
import jax
import jax.numpy as jnp
from jax import lax
from jax.sharding import PartitionSpec as P

HD = 128
SPAN = 2


inverse_temp = 10.0
loss_scale = 2.0**24
norm_eps = 1e-06


def from_behind(x, axis, by):
    devices = lax.axis_size(axis)
    pairs = [(i, i + by) for i in range(devices) if 0 <= i + by < devices]
    return lax.ppermute(x, axis, pairs)


def shards(query_states, key_states, value_states, lengths, queue_keys, write_pos, teacher):
    docs_here, row_count, width = query_states.shape
    kv_width = key_states.shape[2]
    heads_kv = kv_width // HD
    grouped = query_states.reshape(docs_here, row_count, heads_kv, -1, HD)
    score_scale = HD ** (-0.5)
    ctx_index = lax.axis_index("ctx")
    query_pos = ctx_index * row_count + jnp.arange(row_count, dtype=jnp.int32)
    window_rows = SPAN * row_count
    kv_pair = jnp.stack((key_states, value_states))
    kv_blocks = [kv_pair]
    moving = kv_pair
    for offset in range(SPAN):
        moving = from_behind(moving, "ctx", 1)
        kv_blocks.append(moving)
    weights = []
    denominator = 0.0
    numerator = 0.0
    for offset in range(SPAN + 1):
        key_tile = kv_blocks[offset][0].reshape(docs_here, row_count, heads_kv, HD)
        value_tile = kv_blocks[offset][1].reshape(docs_here, row_count, heads_kv, HD)
        key_pos = (ctx_index - offset) * row_count + jnp.arange(row_count, dtype=jnp.int32)
        visible = (
            (key_pos[None, :] <= query_pos[:, None])
            & (key_pos[None, :] > query_pos[:, None] - window_rows)
            & (key_pos[None, :] >= 0)
        )
        scores = (
            jnp.einsum("dqkgh,dtkh->dkgqt", grouped, key_tile, preferred_element_type=jnp.float32)
            * score_scale
        )
        weight = jnp.where(visible, jnp.exp(scores), 0.0)
        weights.append(weight)
        denominator = denominator + jnp.sum(weight, -1)
        numerator = numerator + jnp.einsum(
            "dkgqt,dtkh->dkgqh",
            weight.astype(jnp.bfloat16),
            value_tile,
            preferred_element_type=jnp.float32,
        )
    output = numerator / denominator[..., None]
    live_rows = (query_pos[None, :] < lengths[:, None])[:, None, None, :, None]
    length_float = lengths[:, None].astype(jnp.float32)
    pooled = jnp.sum(jnp.where(live_rows, output, 0.0), 3).reshape(docs_here, -1) / length_float
    target = jnp.exp(teacher)
    summed = lax.psum(pooled, "ctx")
    root_mean = jnp.sqrt(jnp.mean(summed * summed, -1, keepdims=True) + norm_eps)
    norm_scale = root_mean * width**0.5
    unit_vec = summed / norm_scale
    every_unit = lax.all_gather(unit_vec.astype(jnp.bfloat16), "grp", axis=0, tiled=True)
    entry_count = queue_keys.shape[0]
    entry_ids = lax.axis_index(("ctx", "grp")) * entry_count + jnp.arange(
        entry_count, dtype=jnp.int32
    )
    written = entry_ids[:, None] == write_pos[None, :]
    replaced = jnp.dot(
        written.astype(jnp.bfloat16), every_unit, preferred_element_type=jnp.float32
    ).astype(jnp.bfloat16)
    effective = jnp.where(jnp.any(written, 1)[:, None], replaced, queue_keys)
    logits = jnp.dot(every_unit, effective.T, preferred_element_type=jnp.float32) * inverse_temp
    student = jnp.exp(logits)
    cross_part = jnp.sum(target * (teacher - logits), 1)
    student_total, target_total, cross_total = lax.psum(
        (jnp.sum(student, 1), jnp.sum(target, 1), cross_part), ("ctx", "grp")
    )
    loss_value = jnp.mean(
        cross_total / target_total - jnp.log(target_total) + jnp.log(student_total)
    )
    doc_count = every_unit.shape[0]
    grad_logits = (
        loss_scale * (student / student_total[:, None] - target / target_total[:, None]) / doc_count
    )
    unit_part = (
        jnp.dot(grad_logits.astype(jnp.bfloat16), effective, preferred_element_type=jnp.float32)
        * inverse_temp
    )
    grad_all = lax.psum(unit_part, ("ctx", "grp"))
    unit_grad = lax.dynamic_slice_in_dim(grad_all, lax.axis_index("grp") * docs_here, docs_here, 0)
    embedding_grad = (
        unit_grad - unit_vec * jnp.sum(unit_vec * unit_grad, -1, keepdims=True)
    ) / norm_scale
    cotangent = (embedding_grad / length_float).reshape(docs_here, heads_kv, -1, HD)
    cot_round = cotangent.astype(jnp.bfloat16)
    row_dot = jnp.sum(cotangent[:, :, :, None, :] * output, -1)
    query_grad = 0.0
    tile_grads = []
    for offset in range(SPAN + 1):
        key_tile = kv_blocks[offset][0].reshape(docs_here, row_count, heads_kv, HD)
        value_tile = kv_blocks[offset][1].reshape(docs_here, row_count, heads_kv, HD)
        attn_prob = jnp.where(live_rows, weights[offset] / denominator[..., None], 0.0)
        prob_grad = jnp.einsum(
            "dkgh,dtkh->dkgt", cot_round, value_tile, preferred_element_type=jnp.float32
        )
        score_grad = attn_prob * (prob_grad[:, :, :, None, :] - row_dot[..., None])
        score_round = score_grad.astype(jnp.bfloat16)
        query_grad = query_grad + jnp.einsum(
            "dkgqt,dtkh->dqkgh", score_round, key_tile, preferred_element_type=jnp.float32
        )
        key_part = (
            jnp.einsum(
                "dkgqt,dqkgh->dtkh", score_round, grouped, preferred_element_type=jnp.float32
            )
            * score_scale
        )
        value_part = jnp.einsum(
            "dkgqt,dkgh->dtkh",
            attn_prob.astype(jnp.bfloat16),
            cot_round,
            preferred_element_type=jnp.float32,
        )
        tile_grads.append(
            jnp.stack((key_part, value_part)).reshape(2, docs_here, row_count, kv_width)
        )
    kv_grad = tile_grads[SPAN]
    for offset in range(SPAN - 1, -1, -1):
        kv_grad = from_behind(kv_grad, "ctx", -1) + tile_grads[offset]
    query_out = (query_grad * score_scale).reshape(docs_here, row_count, width).astype(jnp.bfloat16)
    return (
        loss_value,
        unit_vec,
        query_out,
        kv_grad[0].astype(jnp.bfloat16),
        kv_grad[1].astype(jnp.bfloat16),
    )


def solution(mesh):
    placed = (
        P("grp", "ctx", None),
        P("grp", "ctx", None),
        P("grp", "ctx", None),
        P("grp"),
        P(("ctx", "grp"), None),
        P(),
        P(None, ("ctx", "grp")),
    )
    return jax.shard_map(
        shards,
        mesh=mesh,
        in_specs=placed,
        out_specs=(
            P(),
            P("grp", None),
            P("grp", "ctx", None),
            P("grp", "ctx", None),
            P("grp", "ctx", None),
        ),
        check_vma=False,
    )
```

profile of v0, /device:TPU:1, one launch (start us, length us, event | category | flops | bytes accessed | tf_op | source)
XLA Modules:
  0.0 779.7 jit_solution(1559296049990210191)
XLA Ops:
  7.2 0.0 all-reduce.3.cloned.1.call-start
  7.2 1.1 copy.112
  8.4 1.0 copy.113
  9.4 0.0 copy-start.29
  9.4 4.9 collective-permute-start
  14.5 0.3 copy.180
  14.8 0.0 copy-start
  14.8 0.1 copy.152
  15.0 0.0 copy-start.8
  15.7 0.6 compare_reduce_fusion
  16.3 0.2 and_and_fusion
  16.5 0.4 fusion.50
  16.9 0.3 fusion.22
  17.3 1.3 collective-permute-done
  18.7 0.4 fusion.51
  19.1 3.4 collective-permute-start.1
  22.5 0.4 convolution_add_fusion.3
  22.9 2.9 collective-permute-done.1
  25.9 0.4 fusion.49
  26.3 1.5 convert_reduce_fusion
  27.8 1.6 select_reduce_fusion
  29.4 137.8 %psum.35 = f32[1,2048]{1,0:T(1,128)S(1)} all-reduce(f32[1,2048]{1,0:T(1,128)S(1)} %bitcast.220), channel_id=1, replica_groups=mesh['ctx'=64,'grp'=8] {'ctx'}, use_global_device_ids=true, to_apply=%region_4.5 | all-reduce | flops 2048 | bytes 16384 | tf_op jit(solution)/shard_map/psum | solution.py:66
  167.2 0.6 multiply_reduce_fusion.3
  168.5 0.0 copy-start.15
  168.5 22.1 %all-gather = bf16[8,1,2048]{2,1,0:T(2,128)(2,1)S(1)} all-gather(bf16[1,1,2048]{2,1,0:T(2,128)(2,1)S(1)} %get-tuple-element.34), channel_id=1, replica_groups=mesh['ctx'=64,'grp'=8] {'grp'}, dimensions={0}, use_global_device_ids=true | all-gather | bytes 36864 | tf_op jit(solution)/shard_map/all_gather | solution.py:70
  190.6 1.8 fusion
  192.4 1.7 multiply_reduce_fusion.2
  194.1 110.9 %all-reduce = (f32[8]{0:T(128)}, f32[8]{0:T(128)}, f32[8]{0:T(128)}) all-reduce(f32[8]{0:T(128)} %get-tuple-element.29, f32[8]{0:T(128)} %get-tuple-element.30, f32[8]{0:T(128)} %get-tuple-element.28), channel_id=1, replica_groups=mesh['ctx'=64,'grp'=8] {'ctx','grp'}, use_global_device_ids=true, to_apply=%region_12.13 | all-reduce | flops 24 | bytes 192 | tf_op jit(solution)/shard_map/psum | solution.py:83
  305.0 1.6 convolution_multiply_fusion
  306.7 0.0 all-reduce.3.cloned.1.call-update
  306.7 1.4 add_reduce_fusion
  308.7 429.7 %all-reduce.3.cloned.1.call-done = f32[8,2048]{1,0:T(8,128)} async-done(((f32[8,2048]{1,0:T(8,128)}), f32[8,2048]{1,0:T(8,128)}) %all-reduce.3.cloned.1.call-update) | async-done | bytes 65552 | tf_op jit(solution)/shard_map/psum | solution.py:97
  738.4 1.5 multiply_reduce_fusion.1
  739.9 1.5 subtract_divide_fusion
  741.4 0.2 fusion.28
  741.5 1.6 multiply_reduce_fusion
  743.1 0.1 fusion.52
  743.3 0.6 fusion.15
  743.9 0.0 copy-done.25
  743.9 1.3 fusion.14
  745.2 0.1 fusion.53
  745.4 0.6 fusion.13
  745.9 0.0 copy-done.23
  745.9 0.1 copy.131
  746.1 0.2 fusion.54
  746.4 0.1 copy.132
  746.5 0.8 pad_maximum_fusion
  747.3 2.3 collective-permute-start.2
  749.7 0.2 fusion.56
  749.9 0.1 copy.139
  750.1 0.1 copy.140
  750.2 0.1 copy.135
  750.4 0.9 fusion.55
  751.3 0.1 copy.136
  751.4 1.5 convolution_bitcast_fusion
  753.0 5.1 collective-permute-done.2
  758.1 1.9 maximum_add_fusion
  760.1 2.0 collective-permute-start.3
  762.2 0.8 convolution_add_fusion.1
  763.0 0.6 fusion.9
  763.6 1.0 copy.141
  764.6 6.3 collective-permute-done.3
  770.9 0.1 fusion.19
  771.0 0.7 slice_bitcast_fusion
  (77 shorter events, 0.3 us)
Async XLA Ops:
  7.2 7.3 copy-start.6
  7.2 7.3 copy-start.7
  7.2 7.4 copy-start.5
  7.2 731.2 %all-reduce.3.cloned.1.call-start = ((), (), s32[]{:S(2)}) async-start(), calls=%async_computation | async-start | bytes 131072 | tf_op jit(solution)/shard_map/psum | solution.py:97
  9.4 6.3 copy-start.29
  9.4 9.2 %collective-permute-start = (bf16[2,1,128,512]{2,3,1,0:T(8,128)(2,1)S(1)}, bf16[2,1,128,512]{2,3,1,0:T(8,128)(2,1)S(1)}, u32[]{:S(2)}, u32[]{:S(2)}) collective-permute-start(bf16[2,1,128,512]{2,3,1,0:T(8,128)(2,1)S(1)} %pad_maximum_fusion.1), channel_id=1, source_target_pairs={{0,8},{8,16},{16,24},{24,32},{32,40},{40,48},{48,56},{56,64},{64,7... | collective-permute-start | bytes 786440 | tf_op jit(solution)/shard_map/ppermute | solution.py:18
  14.8 11.0 %copy-start = (bf16[1,128,2048]{1,2,0:T(8,128)(2,1)}, bf16[1,128,2048]{1,2,0:T(8,128)(2,1)S(1)}, u32[]{:S(2)}) copy-start(bf16[1,128,2048]{1,2,0:T(8,128)(2,1)S(1)} %copy.180) | copy-start | bytes 1572868
  15.0 2.3 copy-start.8
  15.7 12.1 %copy-start.30 = (pred[128]{0:T(512)(128)(4,1)}, pred[128]{0:T(512)(128)(4,1)S(1)}, u32[]{:S(2)}) copy-start(pred[128]{0:T(512)(128)(4,1)S(1)} %broadcast_compare_fusion.3) | copy-start | bytes 388
  15.7 0.6 copy-start.28
  18.6 3.9 copy-start.10
  19.1 6.7 collective-permute-start.1
  25.8 2.0 copy-start.12
  26.3 1.5 copy-start.2
  26.3 1.5 copy-start.17
  168.5 571.4 %copy-start.15 = (f32[1,2048]{1,0:T(1,128)}, f32[1,2048]{1,0:T(1,128)S(1)}, u32[]{:S(2)}) copy-start(f32[1,2048]{1,0:T(1,128)S(1)} %get-tuple-element.35) | copy-start | bytes 24580
  190.6 1.8 copy-start.16
  306.6 436.6 %copy-start.1 = (bf16[1,128,2048]{1,2,0:T(8,128)(2,1)S(1)}, bf16[1,128,2048]{1,2,0:T(8,128)(2,1)}, u32[]{:S(2)}) copy-start(bf16[1,128,2048]{1,2,0:T(8,128)(2,1)} %copy-done) | copy-start | bytes 1572868
  306.6 436.6 %copy-start.18 = (f32[2,8,128]{2,1,0:T(8,128)S(1)}, f32[2,8,128]{2,1,0:T(8,128)}, u32[]{:S(2)}) copy-start(f32[2,8,128]{2,1,0:T(8,128)} %copy-done.17) | copy-start | bytes 24580
  306.6 436.6 %copy-start.31 = (pred[128]{0:T(512)(128)(4,1)S(1)}, pred[128]{0:T(512)(128)(4,1)}, u32[]{:S(2)}) copy-start(pred[128]{0:T(512)(128)(4,1)} %copy-done.30) | copy-start | bytes 388
  741.5 2.4 copy-start.27
  743.1 2.2 copy-start.21
  743.3 0.6 copy-start.25
  743.9 1.4 copy-start.3
  743.9 1.4 copy-start.32
  745.3 0.6 copy-start.23
  745.4 0.7 copy-start.20
  746.1 3.6 copy-start.19
  746.5 3.7 copy-start.14
  747.3 10.8 %collective-permute-start.2 = (f32[2,1,128,512]{3,2,1,0:T(8,128)}, f32[2,1,128,512]{3,2,1,0:T(8,128)}, u32[]{:S(2)}, u32[]{:S(2)}) collective-permute-start(f32[2,1,128,512]{3,2,1,0:T(8,128)} %pad_maximum_fusion), channel_id=1, source_target_pairs={{8,0},{16,8},{24,16},{32,24},{40,32},{48,40},{56,48},{64,56},{72,6... | collective-permute-start | bytes 1572872 | tf_op jit(solution)/shard_map/ppermute | solution.py:18
  750.1 1.4 copy-start.9
  753.0 9.1 %copy-start.11 = (bf16[1,1,128,512]{2,3,1,0:T(8,128)(2,1)S(1)}, bf16[1,1,128,512]{2,3,1,0:T(8,128)(2,1)}, u32[]{:S(2)}) copy-start(bf16[1,1,128,512]{2,3,1,0:T(8,128)(2,1)} %copy-done.10) | copy-start | bytes 393220
  753.0 9.1 %copy-start.22 = (f32[4,4,128]{2,1,0:T(4,128)S(1)}, f32[4,4,128]{2,1,0:T(4,128)}, u32[]{:S(2)}) copy-start(f32[4,4,128]{2,1,0:T(4,128)} %copy-done.21) | copy-start | bytes 24580
  753.0 9.1 %copy-start.26 = (f32[4,4,128]{2,1,0:T(4,128)S(1)}, f32[4,4,128]{2,1,0:T(4,128)}, u32[]{:S(2)}) copy-start(f32[4,4,128]{2,1,0:T(4,128)} %copy-done.25) | copy-start | bytes 24580
  753.0 9.1 %copy-start.33 = (pred[128]{0:T(512)(128)(4,1)S(1)}, pred[128]{0:T(512)(128)(4,1)}, u32[]{:S(2)}) copy-start(pred[128]{0:T(512)(128)(4,1)} %copy-done.30) | copy-start | bytes 388
  760.1 2.9 copy-start.4
  760.1 2.9 copy-start.13
  760.1 2.9 copy-start.24
  760.1 10.8 %collective-permute-start.3 = (f32[2,1,128,512]{3,2,1,0:T(8,128)}, f32[2,1,128,512]{3,2,1,0:T(8,128)S(1)}, u32[]{:S(2)}, u32[]{:S(2)}) collective-permute-start(f32[2,1,128,512]{3,2,1,0:T(8,128)} %maximum_add_fusion), channel_id=1, source_target_pairs={{8,0},{16,8},{24,16},{32,24},{40,32},{48,40},{56,48},{64,56},{72,6... | collective-permute-start | bytes 1572872 | tf_op jit(solution)/shard_map/ppermute | solution.py:18
Sparse Core Ops, SparseCore 0:
  306.8 431.5 all-reduce.2
where the time goes:
time: 782 us; the launch traced here: 780 us
  waiting for transfers between devices  445 us (57%)
  blocking collectives  271 us (35%)
  between operations  17.9 us (2%)
  matrix products  15.8 us (2%)
  starting transfers between devices  12.8 us (2%)
  other arithmetic  11.8 us (2%)
    psum x1, waiting for transfers between devices, shards(): grad_all = lax.psum(unit_part, ('ctx', 'grp'))  430 us
    psum x1, blocking collectives, shards(): summed = lax.psum(pooled, 'ctx')  138 us
    psum x1, blocking collectives, shards(): lax.psum((jnp.sum(student, 1), jnp.sum(target, 1), cross_part), ('ctx', '...  111 us
    all_gather x1, blocking collectives, shards(): lax.all_gather(unit_vec.astype(jnp.bfloat16), 'grp', axis=0, tiled=True)  22.1 us
    ppermute x4, waiting for transfers between devices, from_behind(): return lax.ppermute(x, axis, pairs)  15.7 us
  transfers between devices with their start and end apart: 5, of which 5 were waited for; matrix products, arithmetic and copies ran while one was open for 1% of the time, Pallas kernels for 0%

commit v1 on v0

--- a/solution.py
+++ b/solution.py
@@ -1,21 +1,362 @@
+import functools
+
 import jax
 import jax.numpy as jnp
 from jax import lax
+from jax.experimental import pallas as pl
+from jax.experimental.pallas import tpu as pltpu
 from jax.sharding import PartitionSpec as P
 
 HD = 128
 SPAN = 2
-
+HEADS = 16
+HALF = 8
+DOCS = 8
+ENTRIES = 256
+EXT = ENTRIES + 128
+NZ = 16
+PLANE = 32
+ROWS = 10
 
 inverse_temp = 10.0
 loss_scale = 2.0**24
 norm_eps = 1e-06
+
+MESH = pl.DeviceIdType.MESH
 
 
 def from_behind(x, axis, by):
     devices = lax.axis_size(axis)
     pairs = [(i, i + by) for i in range(devices) if 0 <= i + by < devices]
     return lax.ppermute(x, axis, pairs)
+
+
+def position():
+    ctx = lax.axis_index("ctx")
+    grp = lax.axis_index("grp")
+    return ctx // 32, (ctx // 2) % NZ, ctx % 2, grp
+
+
+def device(x_hi, z, core, grp):
+    return ((x_hi * NZ + z) * 2 + core, grp)
+
+
+def plane_peer(step):
+    x_hi, z, core, grp = position()
+    turn = (step // 4) % 4
+    turn = turn + turn // 2 - 2 * (turn // 3)
+    px = (x_hi + step // 16) % 2
+    pc = (core + step % 2) % 2
+    pl_x = (grp // 4 + (step // 2) % 2) % 2
+    py = (grp + turn) % 4
+    return px, pc, pl_x * 4 + py
+
+
+def z_offset(step):
+    return 8 + ((step + 1) // 2) * (2 * (step % 2) - 1)
+
+
+def send_plane(src_of, dst, send_sem, recv_sem):
+    x_hi, z, core, grp = position()
+    mine = x_hi * 16 + core * 8 + grp
+
+    def one(k, carry):
+        px, pc, pg = plane_peer(31 - k)
+        pltpu.make_async_remote_copy(
+            src_ref=src_of(pc, pg),
+            dst_ref=dst(mine),
+            send_sem=send_sem,
+            recv_sem=recv_sem,
+            device_id=device(px, z, pc, pg),
+            device_id_type=MESH,
+        ).start()
+        return carry
+
+    lax.fori_loop(0, PLANE - 1, one, 0)
+
+
+def send_ring(src, dst, send_sem, recv_sem):
+    x_hi, z, core, grp = position()
+
+    def one(k, carry):
+        pltpu.make_async_remote_copy(
+            src_ref=src,
+            dst_ref=dst(z),
+            send_sem=send_sem,
+            recv_sem=recv_sem,
+            device_id=device(x_hi, (z + z_offset(k)) % NZ, core, grp),
+            device_id_type=MESH,
+        ).start()
+        return carry
+
+    lax.fori_loop(0, NZ - 1, one, 0)
+
+
+def core_copy(src, dst, send_sem, recv_sem):
+    x_hi, z, core, grp = position()
+    return pltpu.make_async_remote_copy(
+        src_ref=src,
+        dst_ref=dst,
+        send_sem=send_sem,
+        recv_sem=recv_sem,
+        device_id=device(x_hi, z, 1 - core, grp),
+        device_id_type=MESH,
+    )
+
+
+def wait_bytes(ref, sem):
+    pltpu.make_async_copy(ref, ref, sem).wait()
+
+
+def sum_slots(ref, count):
+    total = ref[0]
+    for i in range(1, count):
+        total = total + ref[i]
+    return total
+
+
+def two_halves(x):
+    high = x.astype(jnp.bfloat16).astype(jnp.float32)
+    return jnp.concatenate([high, x - high], 0).astype(jnp.bfloat16)
+
+
+def queue_kernel(
+    pos_ref, len_ref, pooled_ref, queue_ref, teacher_ref,
+    emb_ref, cot_ref, loss_ref,
+    eff, mix, core_buf, zb, pb, t_out, tp, tz, t_own, t_half, s_out, ep, ez, e_half, half_sum, ring_out,
+    t_ring_out, t_full, unit_rows, e_ring_out,
+    ready, load_sem, send, recv,
+):
+    x_hi, z, core, grp = position()
+    mine = x_hi * 16 + core * 8 + grp
+    barrier = pltpu.get_barrier_semaphore()
+
+    def hello_plane(k, carry):
+        px, pc, pg = plane_peer(k + 1)
+        pl.semaphore_signal(barrier, inc=1, device_id=device(px, z, pc, pg), device_id_type=MESH)
+        return carry
+
+    def hello_ring(k, carry):
+        to = (z + NZ - 4 + k + k // 4) % NZ
+        pl.semaphore_signal(barrier, inc=1, device_id=device(x_hi, to, core, grp), device_id_type=MESH)
+        return carry
+
+    lax.fori_loop(0, 8, hello_ring, 0)
+    lax.fori_loop(0, PLANE - 1, hello_plane, 0)
+    load = pltpu.make_async_copy(queue_ref, eff.at[pl.ds(0, ENTRIES)], load_sem)
+    load.start()
+    eff[pl.ds(ENTRIES, 128)] = jnp.zeros((128, 2048), jnp.bfloat16)
+
+    base = ((x_hi * NZ + z) * 2 + core) * (8 * ENTRIES) + grp * ENTRIES
+    entry = lax.broadcasted_iota(jnp.int32, (DOCS, ENTRIES), 1) + base
+    lane = lax.broadcasted_iota(jnp.int32, (DOCS, 128), 1)
+    row = lax.broadcasted_iota(jnp.int32, (DOCS, 128), 0)
+    teacher = teacher_ref[...]
+    kept = jnp.ones((DOCS, ENTRIES), jnp.float32)
+    there = jnp.zeros((DOCS, 128), jnp.float32)
+    teacher_at = jnp.zeros((DOCS, 128), jnp.float32)
+    for d in range(DOCS):
+        hit = (entry == pos_ref[d]).astype(jnp.float32)
+        kept = kept - hit
+        at = (lane == d).astype(jnp.float32)
+        there = there + at * jnp.sum(hit, 1, keepdims=True)
+        teacher_at = teacher_at + at * jnp.sum(teacher * hit, 1, keepdims=True)
+    target = jnp.where(kept > 0, jnp.exp(teacher), 0.0)
+    target_at = jnp.where(there > 0, jnp.exp(teacher_at), 0.0)
+    target_sum = jnp.sum(target, 1, keepdims=True) + jnp.sum(target_at, 1, keepdims=True)
+    sum_row = jnp.sum(jnp.where(lane == row, target_sum, 0.0), 0, keepdims=True)
+
+    def spread(out, part):
+        for h in range(HEADS):
+            out[:, h // HALF, h % HALF] = part[:, h * HD : (h + 1) * HD]
+
+    load.wait()
+    mixed = jnp.dot(two_halves(target), eff[pl.ds(0, ENTRIES)], preferred_element_type=jnp.float32)
+    spread(t_out, mixed[:DOCS] + mixed[DOCS:])
+    for c in range(2):
+        t_out[:, c, HALF] = target_at
+        for d in range(DOCS):
+            t_out[d, c, pl.ds(HALF + 1, 1)] = sum_row
+
+    pl.semaphore_wait(barrier, PLANE - 1 + 8)
+    for to in (4, NZ - 4):
+        pl.semaphore_signal(ready, inc=1, device_id=device(x_hi, (z + to) % NZ, core, grp), device_id_type=MESH)
+
+    send_plane(
+        lambda pc, pg: t_out.at[pg, pc, pl.ds(0, ROWS)], lambda me: tp.at[me, pl.ds(0, ROWS)], send.at[0], recv.at[0]
+    )
+    tp[mine] = t_out[grp, core]
+
+    pair = core_copy(pooled_ref.at[pl.ds((1 - core) * HALF, HALF)], core_buf, send.at[1], recv.at[1])
+    pair.start()
+    pl.semaphore_wait(ready, 2)
+    pair.wait_recv()
+    half_sum[...] = pooled_ref[pl.ds(core * HALF, HALF)] + core_buf[...]
+    send_ring(half_sum, lambda me: zb.at[me], send.at[2], recv.at[2])
+    zb[z] = half_sum[...]
+
+    wait_bytes(tp.at[pl.ds(0, PLANE - 1), pl.ds(0, ROWS)], recv.at[0])
+    t_ring_out[...] = sum_slots(tp, PLANE)
+    send_ring(t_ring_out.at[pl.ds(0, ROWS)], lambda me: tz.at[me, pl.ds(0, ROWS)], send.at[3], recv.at[3])
+    tz[z] = t_ring_out[...]
+
+    wait_bytes(zb.at[pl.ds(0, NZ - 1)], recv.at[2])
+    ring_out[...] = sum_slots(zb, NZ)
+    send_plane(lambda pc, pg: ring_out, lambda me: pb.at[me], send.at[4], recv.at[4])
+    pb[mine] = ring_out[...]
+
+    wait_bytes(tz.at[pl.ds(0, NZ - 1), pl.ds(0, ROWS)], recv.at[3])
+    t_own[...] = sum_slots(tz, NZ)
+    t_pair = core_copy(t_own.at[pl.ds(0, HALF)], t_half, send.at[5], recv.at[5])
+    t_pair.start()
+
+    wait_bytes(pb.at[pl.ds(0, PLANE - 1)], recv.at[4])
+    heads = []
+    for c in range(2):
+        both = pb[pl.ds(c * 8, 8)] + pb[pl.ds(16 + c * 8, 8)]
+        unit_rows[:, pl.ds(c * HALF, HALF)] = both
+    square = jnp.zeros((DOCS, HD), jnp.float32)
+    for h in range(HEADS):
+        tile = unit_rows[:, h]
+        heads.append(tile)
+        square = square + tile * tile
+    root_mean = jnp.sqrt(jnp.sum(square, 1, keepdims=True) / 2048.0 + norm_eps)
+    norm_scale = root_mean * 2048.0**0.5
+    for h in range(HEADS):
+        unit = (heads[h] / norm_scale).astype(jnp.bfloat16)
+        eff[pl.ds(ENTRIES, 16), h * HD : (h + 1) * HD] = jnp.concatenate([unit, jnp.zeros_like(unit)], 0)
+    unit16 = eff[pl.ds(ENTRIES, 16)]
+    logits = (
+        lax.dot_general(unit16, eff[...], (((1,), (1,)), ((), ())), preferred_element_type=jnp.float32)[:DOCS]
+        * inverse_temp
+    )
+    near, far = logits[:, :ENTRIES], logits[:, ENTRIES:]
+    student = jnp.where(kept > 0, jnp.exp(near), 0.0)
+    student_at = jnp.where(there > 0, jnp.exp(far), 0.0)
+    student_sum = jnp.sum(student, 1, keepdims=True) + jnp.sum(student_at, 1, keepdims=True)
+    cross = jnp.sum(target * (teacher - near), 1, keepdims=True) + jnp.sum(
+        target_at * (teacher_at - far), 1, keepdims=True
+    )
+    student_row = jnp.sum(jnp.where(lane == row, student_sum, 0.0), 0, keepdims=True)
+    cross_row = jnp.sum(jnp.where(lane == row, cross, 0.0), 0, keepdims=True)
+    mixed = jnp.dot(
+        two_halves(jnp.concatenate([student, student_at], 1)), eff[...], preferred_element_type=jnp.float32
+    )
+    spread(s_out, mixed[:DOCS] + mixed[DOCS:])
+    extra = jnp.concatenate([student_row, cross_row], 0)
+    for c in range(2):
+        for d in range(DOCS):
+            s_out[d, c, pl.ds(HALF, 2)] = extra
+    send_plane(
+        lambda pc, pg: s_out.at[pg, pc, pl.ds(0, ROWS)], lambda me: ep.at[me, pl.ds(0, ROWS)], send.at[6], recv.at[6]
+    )
+    ep[mine] = s_out[grp, core]
+
+    own = unit_rows[grp]
+    own_mean = jnp.sqrt(jnp.sum(jnp.sum(own * own, 1, keepdims=True), 0, keepdims=True) / 2048.0 + norm_eps)
+    own_scale = own_mean * 2048.0**0.5
+    emb = own / own_scale
+    emb_ref[...] = emb
+    t_pair.wait_recv()
+    t_full[pl.ds(core * HALF, HALF)] = t_own[pl.ds(0, HALF)]
+    t_full[pl.ds((1 - core) * HALF, HALF)] = t_half[...]
+    t_sum = t_full[...]
+    lane1 = lax.broadcasted_iota(jnp.int32, (1, 128), 1)
+    at_row = t_own[pl.ds(HALF, 1)]
+    target_row = t_own[pl.ds(HALF + 1, 1)]
+    for d in range(DOCS):
+        weight = jnp.sum(jnp.where(lane1 == d, at_row, 0.0), 1, keepdims=True)
+        other = unit_rows[d]
+        other_mean = jnp.sqrt(jnp.sum(jnp.sum(other * other, 1, keepdims=True), 0, keepdims=True) / 2048.0 + norm_eps)
+        other_unit = (other / (other_mean * 2048.0**0.5)).astype(jnp.bfloat16).astype(jnp.float32)
+        t_sum = t_sum + weight * other_unit
+    target_total = jnp.sum(jnp.where(lane1 == grp, target_row, 0.0), 1, keepdims=True)
+
+    wait_bytes(ep.at[pl.ds(0, PLANE - 1), pl.ds(0, ROWS)], recv.at[6])
+    e_ring_out[...] = sum_slots(ep, PLANE)
+    send_ring(e_ring_out.at[pl.ds(0, ROWS)], lambda me: ez.at[me, pl.ds(0, ROWS)], send.at[7], recv.at[7])
+    ez[z] = e_ring_out[...]
+    wait_bytes(ez.at[pl.ds(0, NZ - 1), pl.ds(0, ROWS)], recv.at[7])
+    half_sum2 = sum_slots(ez, NZ)
+    mix[...] = half_sum2
+    e_pair = core_copy(mix.at[pl.ds(0, HALF)], e_half, send.at[8], recv.at[8])
+    e_pair.start()
+    student_all = mix[pl.ds(HALF, 1)]
+    cross_all = mix[pl.ds(HALF + 1, 1)]
+    student_total = jnp.sum(jnp.where(lane1 == grp, student_all, 0.0), 1, keepdims=True)
+    terms = jnp.where(
+        lane1 < DOCS,
+        cross_all / jnp.where(lane1 < DOCS, target_row, 1.0)
+        - jnp.log(jnp.where(lane1 < DOCS, target_row, 1.0))
+        + jnp.log(jnp.where(lane1 < DOCS, student_all, 1.0)),
+        0.0,
+    )
+    loss_ref[...] = jnp.sum(terms, 1, keepdims=True) / DOCS
+    e_pair.wait_recv()
+    ring_full = t_full
+    ring_full[pl.ds(core * HALF, HALF)] = mix[pl.ds(0, HALF)]
+    ring_full[pl.ds((1 - core) * HALF, HALF)] = e_half[...]
+    unit_grad = (
+        inverse_temp * loss_scale / DOCS * (ring_full[...] / student_total - t_sum / target_total)
+    )
+    inner = jnp.sum(jnp.sum(emb * unit_grad, 1, keepdims=True), 0, keepdims=True)
+    cot_ref[...] = (unit_grad - emb * inner) / own_scale / len_ref[0].astype(jnp.float32)
+
+    wait_bytes(tp.at[pl.ds(0, PLANE - 1), pl.ds(0, ROWS)], send.at[0])
+    pair.wait_send()
+    wait_bytes(zb.at[pl.ds(0, NZ - 1)], send.at[2])
+    wait_bytes(tz.at[pl.ds(0, NZ - 1), pl.ds(0, ROWS)], send.at[3])
+    wait_bytes(pb.at[pl.ds(0, PLANE - 1)], send.at[4])
+    t_pair.wait_send()
+    wait_bytes(ep.at[pl.ds(0, PLANE - 1), pl.ds(0, ROWS)], send.at[6])
+    wait_bytes(ez.at[pl.ds(0, NZ - 1), pl.ds(0, ROWS)], send.at[7])
+    e_pair.wait_send()
+
+
+def queue_part(pooled, lengths, queue_keys, write_pos, teacher):
+    vmem = pl.BlockSpec(memory_space=pltpu.VMEM)
+    smem = pl.BlockSpec(memory_space=pltpu.SMEM)
+    f32 = lambda *shape: pltpu.VMEM(shape, jnp.float32)
+    return pl.pallas_call(
+        queue_kernel,
+        name="queue_part",
+        out_shape=(
+            jax.ShapeDtypeStruct((HEADS, HD), jnp.float32),
+            jax.ShapeDtypeStruct((HEADS, HD), jnp.float32),
+            jax.ShapeDtypeStruct((1, 1), jnp.float32),
+        ),
+        in_specs=[smem, smem, vmem, pl.BlockSpec(memory_space=pl.ANY), vmem],
+        out_specs=(vmem, vmem, vmem),
+        scratch_shapes=[
+            pltpu.VMEM((EXT, 2048), jnp.bfloat16),
+            f32(16, 128),
+            f32(HALF, 128),
+            f32(NZ, HALF, 128),
+            f32(PLANE, HALF, 128),
+            f32(DOCS, 2, 16, 128),
+            f32(PLANE, 16, 128),
+            f32(NZ, 16, 128),
+            f32(16, 128),
+            f32(HALF, 128),
+            f32(DOCS, 2, 16, 128),
+            f32(PLANE, 16, 128),
+            f32(NZ, 16, 128),
+            f32(HALF, 128),
+            f32(HALF, 128),
+            f32(HALF, 128),
+            f32(16, 128),
+            f32(HEADS, 128),
+            f32(DOCS, HEADS, 128),
+            f32(16, 128),
+            pltpu.SemaphoreType.REGULAR,
+            pltpu.SemaphoreType.DMA,
+            pltpu.SemaphoreType.DMA((9,)),
+            pltpu.SemaphoreType.DMA((9,)),
+        ],
+        compiler_params=pltpu.CompilerParams(
+            collective_id=0, has_side_effects=True, vmem_limit_bytes=32 * 1024 * 1024
+        ),
+    )(write_pos, lengths, pooled, queue_keys, teacher)
 
 
 def shards(query_states, key_states, value_states, lengths, queue_keys, write_pos, teacher):
@@ -62,44 +403,12 @@
     live_rows = (query_pos[None, :] < lengths[:, None])[:, None, None, :, None]
     length_float = lengths[:, None].astype(jnp.float32)
     pooled = jnp.sum(jnp.where(live_rows, output, 0.0), 3).reshape(docs_here, -1) / length_float
-    target = jnp.exp(teacher)
-    summed = lax.psum(pooled, "ctx")
-    root_mean = jnp.sqrt(jnp.mean(summed * summed, -1, keepdims=True) + norm_eps)
-    norm_scale = root_mean * width**0.5
-    unit_vec = summed / norm_scale
-    every_unit = lax.all_gather(unit_vec.astype(jnp.bfloat16), "grp", axis=0, tiled=True)
-    entry_count = queue_keys.shape[0]
-    entry_ids = lax.axis_index(("ctx", "grp")) * entry_count + jnp.arange(
-        entry_count, dtype=jnp.int32
-    )
-    written = entry_ids[:, None] == write_pos[None, :]
-    replaced = jnp.dot(
-        written.astype(jnp.bfloat16), every_unit, preferred_element_type=jnp.float32
-    ).astype(jnp.bfloat16)
-    effective = jnp.where(jnp.any(written, 1)[:, None], replaced, queue_keys)
-    logits = jnp.dot(every_unit, effective.T, preferred_element_type=jnp.float32) * inverse_temp
-    student = jnp.exp(logits)
-    cross_part = jnp.sum(target * (teacher - logits), 1)
-    student_total, target_total, cross_total = lax.psum(
-        (jnp.sum(student, 1), jnp.sum(target, 1), cross_part), ("ctx", "grp")
-    )
-    loss_value = jnp.mean(
-        cross_total / target_total - jnp.log(target_total) + jnp.log(student_total)
-    )
-    doc_count = every_unit.shape[0]
-    grad_logits = (
-        loss_scale * (student / student_total[:, None] - target / target_total[:, None]) / doc_count
-    )
-    unit_part = (
-        jnp.dot(grad_logits.astype(jnp.bfloat16), effective, preferred_element_type=jnp.float32)
-        * inverse_temp
-    )
-    grad_all = lax.psum(unit_part, ("ctx", "grp"))
-    unit_grad = lax.dynamic_slice_in_dim(grad_all, lax.axis_index("grp") * docs_here, docs_here, 0)
-    embedding_grad = (
-        unit_grad - unit_vec * jnp.sum(unit_vec * unit_grad, -1, keepdims=True)
-    ) / norm_scale
-    cotangent = (embedding_grad / length_float).reshape(docs_here, heads_kv, -1, HD)
+    emb, cot, loss = queue_part(
+        pooled.reshape(HEADS, HD), lengths, queue_keys, write_pos, teacher
+    )
+    unit_vec = emb.reshape(docs_here, width)
+    loss_value = loss[0, 0]
+    cotangent = cot.reshape(docs_here, heads_kv, -1, HD)
     cot_round = cotangent.astype(jnp.bfloat16)
     row_dot = jnp.sum(cotangent[:, :, :, None, :] * output, -1)
     query_grad = 0.0

time: 782 us -> 110 us (0.14)
  the two profiles are of different devices: /device:TPU:1 before, /device:TPU:6 now
where the time goes in v1:
time: 110 us; the launch traced here: 109 us
  Pallas kernels  36.8 us (33%)
  waiting for transfers between devices  26.5 us (24%)
  starting transfers between devices  16.8 us (15%)
  matrix products  10.8 us (10%)
  local copies, waits for them, and re-layouts  9.46 us (9%)
  other arithmetic  5.55 us (5%)
  between operations  3.4 us (3%)
    pallas_call x1, Pallas kernels, queue_part(): pl.pallas_call(queue_kernel, name='queue_part', out_shape=(jax.ShapeDtype...  36.8 us
    ppermute x4, waiting for transfers between devices, from_behind(): return lax.ppermute(x, axis, pairs)  26.5 us
    ppermute x4, starting transfers between devices, from_behind(): return lax.ppermute(x, axis, pairs)  16.8 us
    unnamed x42, local copies, waits for them, and re-layouts  5.53 us
    dot_general x3, matrix products, shards(): jnp.einsum('dkgqt,dqkgh->dtkh', score_round, grouped, preferred_element_t...  4.31 us
    another operation x6, local copies, waits for them, and re-layouts, shards(): jnp.stack((key_part, value_part)).reshape(2, docs_here, row_count, kv_width)  2.69 us
  transfers between devices with their start and end apart: 4, of which 4 were waited for; matrix products, arithmetic and copies ran while one was open for 8% of the time, Pallas kernels for 0%

profile of v1, /device:TPU:6, one launch (start us, length us, event | category | flops | bytes accessed | tf_op | source)
XLA Modules:
  0.0 109.3 jit_solution(14626965042343042731)
XLA Ops:
  0.6 1.1 copy.45
  1.7 0.1 copy.44
  1.8 0.0 copy-start.5
  1.9 2.1 %collective-permute-start = (bf16[2,1,128,512]{2,3,1,0:T(8,128)(2,1)S(1)}, bf16[2,1,128,512]{2,3,1,0:T(8,128)(2,1)S(1)}, u32[]{:S(2)}, u32[]{:S(2)}) collective-permute-start(bf16[2,1,128,512]{2,3,1,0:T(8,128)(2,1)S(1)} %pad_maximum_fusion.1), channel_id=1, source_target_pairs={{0,8},{8,16},{16,24},{24,32},{32,40},{40,48},{48,56},{56,64},{64,7... | collective-permute-start | bytes 786440 | tf_op jit(solution)/shard_map/ppermute | solution.py:31
  4.0 0.0 copy-start.7
  4.1 0.9 copy-done.7
  5.6 0.0 copy-start.17
  5.6 0.3 copy.111
  5.9 0.1 copy.84
  6.1 0.2 and_and_fusion
  6.2 0.4 fusion.38
  6.7 0.4 fusion.21
  7.0 10.7 %collective-permute-done = bf16[2,1,128,512]{2,3,1,0:T(8,128)(2,1)S(1)} collective-permute-done((bf16[2,1,128,512]{2,3,1,0:T(8,128)(2,1)S(1)}, bf16[2,1,128,512]{2,3,1,0:T(8,128)(2,1)S(1)}, u32[]{:S(2)}, u32[]{:S(2)}) %collective-permute-start) | collective-permute-done | bytes 262176 | tf_op jit(solution)/shard_map/ppermute | solution.py:31
  17.8 0.0 copy-start.8
  17.8 0.4 fusion.39
  18.2 0.2 copy-done.8
  18.4 1.9 %collective-permute-start.1 = (bf16[2,1,128,512]{2,3,1,0:T(8,128)(2,1)S(1)}, bf16[2,1,128,512]{2,3,1,0:T(8,128)(2,1)S(1)}, u32[]{:S(2)}, u32[]{:S(2)}) collective-permute-start(bf16[2,1,128,512]{2,3,1,0:T(8,128)(2,1)S(1)} %collective-permute-done), channel_id=1, source_target_pairs={{0,8},{8,16},{16,24},{24,32},{32,40},{40,48},{48,56},{56,64},{64,7... | collective-permute-start | bytes 786440 | tf_op jit(solution)/shard_map/ppermute | solution.py:31
  20.3 0.3 convolution_add_fusion.3
  20.7 9.0 %collective-permute-done.1 = bf16[2,1,128,512]{2,3,1,0:T(8,128)(2,1)S(1)} collective-permute-done((bf16[2,1,128,512]{2,3,1,0:T(8,128)(2,1)S(1)}, bf16[2,1,128,512]{2,3,1,0:T(8,128)(2,1)S(1)}, u32[]{:S(2)}, u32[]{:S(2)}) %collective-permute-start.1) | collective-permute-done | bytes 262176 | tf_op jit(solution)/shard_map/ppermute | solution.py:31
  29.7 0.0 copy-start.10
  29.8 0.4 fusion.37
  30.2 0.2 copy-done.10
  30.4 1.5 %convert_reduce_fusion = (bf16[4,4,128]{2,1,0:T(4,128)(2,1)S(1)}, bf16[4,4,128]{2,1,0:T(4,128)(2,1)S(1)}, bf16[4,4,128]{2,1,0:T(4,128)(2,1)}) fusion(f32[1,4,4,128,128]{3,4,2,1,0:T(8,128)S(1)} %get-tuple-element.36, f32[4,4,128]{2,1,0:T(4,128)S(1)} %bitcast.202, pred[128]{0:T(512)(128)(4,1)S(1)} %broadcast_compare_fusion.3, ...), kind=kLoop, calls=%fused_computation.26 | loop fusion | flops 3926016 | bytes 3166336 | tf_op jit(solution)/shard_map/dkgqt,dkgh->dtkh/reduce_sum | solution.py:434
  31.9 0.0 copy-done.17
  31.9 0.5 select_reduce_fusion
  32.5 0.0 copy-start.1
  32.5 0.0 copy-start.2
  32.5 0.6 copy-done
  33.1 0.1 copy-done.1
  33.2 36.8 %queue_part.1 = (f32[16,128]{1,0:T(8,128)S(1)}, f32[16,128]{1,0:T(8,128)S(1)}, f32[1,1]{1,0:T(1,128)}) custom-call(s32[8]{0:T(128)S(1)} %copy-done.2, s32[1]{0:T(128)} %copy.118.len_ref, f32[16,128]{1,0:T(8,128)S(1)} %bitcast.175, bf16[256,2048]{1,0:T(8,128)(2,1)S(1)} %copy-done, f32[8,256]{1,0:T(8,128)S(1)} %copy-done.1), custom_call_target="tpu_custom_call" | custom-call | tf_op jit(solution)/shard_map/queue_part/pallas_call | solution.py:320
  70.1 1.0 multiply_reduce_fusion
  71.1 0.8 fusion.27
  71.8 0.1 fusion.40
  72.0 0.1 fusion.41
  72.1 0.3 fusion.42
  72.4 0.0 copy-start.18
  72.4 0.1 copy.64
  72.5 0.5 copy-done.13
  73.1 2.5 %fusion.12 = f32[4,128,128]{1,2,0:T(8,128)} fusion(bf16[128,4,4,128]{0,3,2,1:T(8,128)(2,1)S(1)} %bitcast.180, f32[4,4,128]{2,1,0:T(4,128)S(1)} %fusion.41, f32[4,4,128]{2,1,0:T(4,128)S(1)} %copy-done.13, f32[1,4,4,128,128]{3,4,2,1,0:T(8,128)} %copy-done.3, f32[4,4,128]{2,1,0:T(4,128)S(1)} %bitcast.204, pred[128]{0:T(512)(128)(4,1)S(1)} %copy-done.18), kind=kOutput, calls=%fused_computation.23 | convolution fusion | flops 68485120 | bytes 1859712 | tf_op jit(solution)/shard_map/dkgqt,dqkgh->dtkh/dot_general | solution.py:429
  75.6 1.1 copy.63
  76.7 0.8 pad_maximum_fusion
  77.5 5.4 %collective-permute-start.2 = (f32[2,1,128,512]{3,2,1,0:T(8,128)}, f32[2,1,128,512]{3,2,1,0:T(8,128)}, u32[]{:S(2)}, u32[]{:S(2)}) collective-permute-start(f32[2,1,128,512]{3,2,1,0:T(8,128)} %pad_maximum_fusion), channel_id=1, source_target_pairs={{8,0},{16,8},{24,16},{32,24},{40,32},{48,40},{56,48},{64,56},{72,6... | collective-permute-start | bytes 1572872 | tf_op jit(solution)/shard_map/ppermute | solution.py:31
  82.9 0.2 fusion.43
  83.2 0.1 copy.68
  83.3 1.3 %fusion.13 = f32[4,128,128]{1,2,0:T(8,128)} fusion(bf16[128,4,4,128]{0,3,2,1:T(8,128)(2,1)S(1)} %bitcast.181, f32[4,4,128]{2,1,0:T(4,128)S(1)} %fusion.40, f32[4,4,128]{2,1,0:T(4,128)S(1)} %copy-done.13, f32[1,4,4,128,128]{3,4,2,1,0:T(8,128)S(1)} %get-tuple-element.38, f32[4,4,128]{2,1,0:T(4,128)S(1)} %bitcast.205, pred[128]{0:T(512)(128)(4,1)S(1)} %copy-done.18), kind=kOutput, calls=%fused_computation.24 | convolution fusion | flops 68485120 | bytes 1859712 | tf_op jit(solution)/shard_map/dkgqt,dqkgh->dtkh/dot_general | solution.py:429
  84.6 1.1 copy.67
  85.7 0.0 copy-start.9
  85.7 0.8 convolution_bitcast_fusion
  86.5 0.1 copy-done.9
  86.6 0.8 convolution_add_fusion.1
  87.4 0.0 copy-start.11
  87.4 2.5 %collective-permute-done.2 = f32[2,1,128,512]{3,2,1,0:T(8,128)} collective-permute-done((f32[2,1,128,512]{3,2,1,0:T(8,128)}, f32[2,1,128,512]{3,2,1,0:T(8,128)}, u32[]{:S(2)}, u32[]{:S(2)}) %collective-permute-start.2) | collective-permute-done | bytes 524320 | tf_op jit(solution)/shard_map/ppermute | solution.py:31
  89.9 1.9 %maximum_add_fusion = f32[2,1,128,512]{3,2,1,0:T(8,128)} fusion(f32[2,1,128,512]{3,2,1,0:T(8,128)} %collective-permute-done.2, f32[1,1,128,512]{3,2,1,0:T(8,128)S(1)} %copy.68, f32[1,1,128,512]{3,2,1,0:T(8,128)S(1)} %copy.67), kind=kLoop, calls=%fused_computation.41 | loop fusion | flops 262144 | bytes 1572864 | tf_op jit(solution)/shard_map/add | solution.py:445
  91.8 7.4 %collective-permute-start.3 = (f32[2,1,128,512]{3,2,1,0:T(8,128)}, f32[2,1,128,512]{3,2,1,0:T(8,128)S(1)}, u32[]{:S(2)}, u32[]{:S(2)}) collective-permute-start(f32[2,1,128,512]{3,2,1,0:T(8,128)} %maximum_add_fusion), channel_id=1, source_target_pairs={{8,0},{16,8},{24,16},{32,24},{40,32},{48,40},{56,48},{64,56},{72,6... | collective-permute-start | bytes 1572872 | tf_op jit(solution)/shard_map/ppermute | solution.py:31
  99.3 0.6 fusion.8
  99.8 1.0 copy.73
  100.9 0.2 fusion.44
  101.1 0.1 copy.72
  101.2 0.6 fusion.14
  101.8 0.1 copy.71
  101.9 4.3 %collective-permute-done.3 = f32[2,1,128,512]{3,2,1,0:T(8,128)S(1)} collective-permute-done((f32[2,1,128,512]{3,2,1,0:T(8,128)}, f32[2,1,128,512]{3,2,1,0:T(8,128)S(1)}, u32[]{:S(2)}, u32[]{:S(2)}) %collective-permute-start.3) | collective-permute-done | bytes 524320 | tf_op jit(solution)/shard_map/ppermute | solution.py:31
  106.2 0.1 fusion.18
  106.3 0.7 slice_bitcast_fusion
  107.6 0.6 copy.120
  (33 shorter events, 0.2 us)
Async XLA Ops:
  0.6 1.1 copy-start.6
  1.8 3.8 %copy-start.5 = (bf16[1,128,2048]{2,1,0:T(8,128)(2,1)S(1)}, bf16[1,128,2048]{2,1,0:T(8,128)(2,1)}, u32[]{:S(2)}) copy-start(bf16[1,128,2048]{2,1,0:T(8,128)(2,1)} %param.7) | copy-start | bytes 1572868
  1.9 15.9 %collective-permute-start = (bf16[2,1,128,512]{2,3,1,0:T(8,128)(2,1)S(1)}, bf16[2,1,128,512]{2,3,1,0:T(8,128)(2,1)S(1)}, u32[]{:S(2)}, u32[]{:S(2)}) collective-permute-start(bf16[2,1,128,512]{2,3,1,0:T(8,128)(2,1)S(1)} %pad_maximum_fusion.1), channel_id=1, source_target_pairs={{0,8},{8,16},{16,24},{24,32},{32,40},{40,48},{48,56},{56,64},{64,7... | collective-permute-start | bytes 786440 | tf_op jit(solution)/shard_map/ppermute | solution.py:31
  4.0 0.9 copy-start.7
  5.6 26.3 %copy-start.17 = (pred[128]{0:T(512)(128)(4,1)}, pred[128]{0:T(512)(128)(4,1)S(1)}, u32[]{:S(2)}) copy-start(pred[128]{0:T(512)(128)(4,1)S(1)} %broadcast_compare_fusion.3) | copy-start | bytes 388
  17.8 0.7 copy-start.8
  18.4 11.3 %collective-permute-start.1 = (bf16[2,1,128,512]{2,3,1,0:T(8,128)(2,1)S(1)}, bf16[2,1,128,512]{2,3,1,0:T(8,128)(2,1)S(1)}, u32[]{:S(2)}, u32[]{:S(2)}) collective-permute-start(bf16[2,1,128,512]{2,3,1,0:T(8,128)(2,1)S(1)} %collective-permute-done), channel_id=1, source_target_pairs={{0,8},{8,16},{16,24},{24,32},{32,40},{40,48},{48,56},{56,64},{64,7... | collective-permute-start | bytes 786440 | tf_op jit(solution)/shard_map/ppermute | solution.py:31
  29.7 0.7 copy-start.10
  30.4 1.5 %copy-start.3 = (f32[1,4,4,128,128]{3,4,2,1,0:T(8,128)}, f32[1,4,4,128,128]{3,4,2,1,0:T(8,128)S(1)}, u32[]{:S(2)}) copy-start(f32[1,4,4,128,128]{3,4,2,1,0:T(8,128)S(1)} %get-tuple-element.34) | copy-start | bytes 3145732
  31.9 1.2 %copy-start = (bf16[256,2048]{1,0:T(8,128)(2,1)S(1)}, bf16[256,2048]{1,0:T(8,128)(2,1)}, u32[]{:S(2)}) copy-start(bf16[256,2048]{1,0:T(8,128)(2,1)} %queue_ref.1) | copy-start | bytes 3145732
  32.5 0.8 copy-start.1
  32.5 0.8 copy-start.2
  72.0 11.3 %copy-start.15 = (f32[4,4,128]{2,1,0:T(4,128)}, f32[4,4,128]{2,1,0:T(4,128)S(1)}, u32[]{:S(2)}) copy-start(f32[4,4,128]{2,1,0:T(4,128)S(1)} %fusion.40) | copy-start | bytes 24580
  72.4 0.7 copy-start.13
  72.4 0.7 copy-start.18
  76.7 6.2 %copy-start.12 = (bf16[4,4,128]{2,1,0:T(4,128)(2,1)S(1)}, bf16[4,4,128]{2,1,0:T(4,128)(2,1)}, u32[]{:S(2)}) copy-start(bf16[4,4,128]{2,1,0:T(4,128)(2,1)} %get-tuple-element.23) | copy-start | bytes 12292
  77.5 12.4 %collective-permute-start.2 = (f32[2,1,128,512]{3,2,1,0:T(8,128)}, f32[2,1,128,512]{3,2,1,0:T(8,128)}, u32[]{:S(2)}, u32[]{:S(2)}) collective-permute-start(f32[2,1,128,512]{3,2,1,0:T(8,128)} %pad_maximum_fusion), channel_id=1, source_target_pairs={{8,0},{16,8},{24,16},{32,24},{40,32},{48,40},{56,48},{64,56},{72,6... | collective-permute-start | bytes 1572872 | tf_op jit(solution)/shard_map/ppermute | solution.py:31
  84.6 1.1 %copy-start.14 = (f32[4,4,128]{2,1,0:T(4,128)S(1)}, f32[4,4,128]{2,1,0:T(4,128)}, u32[]{:S(2)}) copy-start(f32[4,4,128]{2,1,0:T(4,128)} %fusion.27) | copy-start | bytes 24580
  85.7 0.9 copy-start.9
  85.7 0.9 copy-start.16
  87.4 11.9 %copy-start.4 = (f32[1,4,4,128,128]{3,4,2,1,0:T(8,128)S(1)}, f32[1,4,4,128,128]{3,4,2,1,0:T(8,128)}, u32[]{:S(2)}) copy-start(f32[1,4,4,128,128]{3,4,2,1,0:T(8,128)} %copy-done.3) | copy-start | bytes 3145732
  87.4 11.9 %copy-start.11 = (bf16[1,1,128,512]{2,3,1,0:T(8,128)(2,1)S(1)}, bf16[1,1,128,512]{2,3,1,0:T(8,128)(2,1)}, u32[]{:S(2)}) copy-start(bf16[1,1,128,512]{2,3,1,0:T(8,128)(2,1)} %copy-done.10) | copy-start | bytes 393220
  91.8 14.4 %collective-permute-start.3 = (f32[2,1,128,512]{3,2,1,0:T(8,128)}, f32[2,1,128,512]{3,2,1,0:T(8,128)S(1)}, u32[]{:S(2)}, u32[]{:S(2)}) collective-permute-start(f32[2,1,128,512]{3,2,1,0:T(8,128)} %maximum_add_fusion), channel_id=1, source_target_pairs={{8,0},{16,8},{24,16},{32,24},{40,32},{48,40},{56,48},{64,56},{72,6... | collective-permute-start | bytes 1572872 | tf_op jit(solution)/shard_map/ppermute | solution.py:31

commit v2 on v1

--- a/solution.py
+++ b/solution.py
@@ -8,8 +8,9 @@
 from jax.sharding import PartitionSpec as P
 
 HD = 128
-SPAN = 2
 HEADS = 16
+GROUPS = 4
+BLOCK = 128
 HALF = 8
 DOCS = 8
 ENTRIES = 256
@@ -23,12 +24,6 @@
 norm_eps = 1e-06
 
 MESH = pl.DeviceIdType.MESH
-
-
-def from_behind(x, axis, by):
-    devices = lax.axis_size(axis)
-    pairs = [(i, i + by) for i in range(devices) if 0 <= i + by < devices]
-    return lax.ppermute(x, axis, pairs)
 
 
 def position():
@@ -120,12 +115,13 @@
     return jnp.concatenate([high, x - high], 0).astype(jnp.bfloat16)
 
 
-def queue_kernel(
-    pos_ref, len_ref, pooled_ref, queue_ref, teacher_ref,
-    emb_ref, cot_ref, loss_ref,
+def whole_kernel(
+    pos_ref, len_ref, query_hbm, key_hbm, value_hbm, queue_ref, teacher_hbm,
+    loss_ref, emb_ref, dq_ref, dk_ref, dv_ref,
+    query, keys, values, teacher_ref, prob, sums, sums_in, dk_out, dk_in, score, pooled_ref,
     eff, mix, core_buf, zb, pb, t_out, tp, tz, t_own, t_half, s_out, ep, ez, e_half, half_sum, ring_out,
     t_ring_out, t_full, unit_rows, e_ring_out,
-    ready, load_sem, send, recv,
+    ready, load_sem, send, recv, near_send, near_recv,
 ):
     x_hi, z, core, grp = position()
     mine = x_hi * 16 + core * 8 + grp
@@ -141,16 +137,32 @@
         pl.semaphore_signal(barrier, inc=1, device_id=device(x_hi, to, core, grp), device_id_type=MESH)
         return carry
 
+    ctx = (x_hi * NZ + z) * 2 + core
+    nearby = {by: ((ctx + 64 + by) % 64, grp) for by in (1, 2, -1, -2)}
     lax.fori_loop(0, 8, hello_ring, 0)
     lax.fori_loop(0, PLANE - 1, hello_plane, 0)
-    load = pltpu.make_async_copy(queue_ref, eff.at[pl.ds(0, ENTRIES)], load_sem)
-    load.start()
+    for to in nearby.values():
+        pl.semaphore_signal(barrier, inc=1, device_id=to, device_id_type=MESH)
+    own_rows = pl.ds(2 * BLOCK, BLOCK)
+    loads = [
+        pltpu.make_async_copy(source, goal, load_sem.at[i])
+        for i, (source, goal) in enumerate((
+            (key_hbm.at[0], keys.at[own_rows]),
+            (value_hbm.at[0], values.at[own_rows]),
+            (teacher_hbm, teacher_ref),
+            (queue_ref, eff.at[pl.ds(0, ENTRIES)]),
+            (query_hbm.at[0], query),
+        ))
+    ]
+    for load in loads:
+        load.start()
     eff[pl.ds(ENTRIES, 128)] = jnp.zeros((128, 2048), jnp.bfloat16)
 
     base = ((x_hi * NZ + z) * 2 + core) * (8 * ENTRIES) + grp * ENTRIES
     entry = lax.broadcasted_iota(jnp.int32, (DOCS, ENTRIES), 1) + base
     lane = lax.broadcasted_iota(jnp.int32, (DOCS, 128), 1)
     row = lax.broadcasted_iota(jnp.int32, (DOCS, 128), 0)
+    loads[2].wait()
     teacher = teacher_ref[...]
     kept = jnp.ones((DOCS, ENTRIES), jnp.float32)
     there = jnp.zeros((DOCS, 128), jnp.float32)
@@ -170,7 +182,7 @@
         for h in range(HEADS):
             out[:, h // HALF, h % HALF] = part[:, h * HD : (h + 1) * HD]
 
-    load.wait()
+    loads[3].wait()
     mixed = jnp.dot(two_halves(target), eff[pl.ds(0, ENTRIES)], preferred_element_type=jnp.float32)
     spread(t_out, mixed[:DOCS] + mixed[DOCS:])
     for c in range(2):
@@ -178,7 +190,22 @@
         for d in range(DOCS):
             t_out[d, c, pl.ds(HALF + 1, 1)] = sum_row
 
-    pl.semaphore_wait(barrier, PLANE - 1 + 8)
+    pl.semaphore_wait(barrier, PLANE - 1 + 8 + 4)
+    loads[0].wait()
+    loads[1].wait()
+    halo = []
+    for i, (held, by) in enumerate(((keys, 1), (keys, 2), (values, 1), (values, 2))):
+        halo.append(
+            pltpu.make_async_remote_copy(
+                src_ref=held.at[own_rows],
+                dst_ref=held.at[pl.ds((2 - by) * BLOCK, BLOCK)],
+                send_sem=near_send.at[i],
+                recv_sem=near_recv.at[i],
+                device_id=nearby[by],
+                device_id_type=MESH,
+            )
+        )
+        halo[-1].start()
     for to in (4, NZ - 4):
         pl.semaphore_signal(ready, inc=1, device_id=device(x_hi, (z + to) % NZ, core, grp), device_id_type=MESH)
 
@@ -186,6 +213,63 @@
         lambda pc, pg: t_out.at[pg, pc, pl.ds(0, ROWS)], lambda me: tp.at[me, pl.ds(0, ROWS)], send.at[0], recv.at[0]
     )
     tp[mine] = t_out[grp, core]
+
+
+    loads[4].wait()
+    later = lax.broadcasted_iota(jnp.int32, (BLOCK, BLOCK), 1)
+    rows = lax.broadcasted_iota(jnp.int32, (BLOCK, BLOCK), 0)
+    seen = (
+        (later > rows) & (ctx >= 2),
+        (later >= 0) & (ctx >= 1),
+        later <= rows,
+    )
+
+    def stacked(g):
+        return jnp.concatenate([query[:, (4 * g + j) * HD : (4 * g + j + 1) * HD] for j in range(4)], 0)
+
+    for block in (2, 1, 0):
+        if block < 2:
+            halo[1 - block].wait_recv()
+        for g in range(GROUPS):
+            tile = keys[pl.ds(block * BLOCK, BLOCK), g * HD : (g + 1) * HD]
+            scores = lax.dot_general(
+                stacked(g), tile, (((1,), (1,)), ((), ())), preferred_element_type=jnp.float32
+            )
+            weight = jnp.exp(scores * HD ** (-0.5)).reshape(4, BLOCK, BLOCK)
+            prob[4 * g : 4 * g + 4, :, block * BLOCK : (block + 1) * BLOCK] = jnp.where(seen[block][None], weight, 0.0)
+
+    length = len_ref[0]
+    place = lax.broadcasted_iota(jnp.int32, (BLOCK, 1), 0) + ctx * BLOCK
+    live = (place < length).astype(jnp.float32)
+    for h in range(HEADS):
+        weight = prob[h]
+        total = weight[:, :BLOCK] + weight[:, BLOCK : 2 * BLOCK] + weight[:, 2 * BLOCK :]
+        part = weight * (live / jnp.sum(total, 1, keepdims=True))
+        prob[h] = part
+        column = jnp.sum(part, 0, keepdims=True)
+        for block in range(3):
+            sums[block, pl.ds(h, 1)] = column[:, block * BLOCK : (block + 1) * BLOCK]
+    sum_copies = []
+    for i, by in enumerate((1, 2)):
+        sum_copies.append(
+            pltpu.make_async_remote_copy(
+                src_ref=sums.at[2 - by],
+                dst_ref=sums_in.at[i],
+                send_sem=near_send.at[4 + i],
+                recv_sem=near_recv.at[4 + i],
+                device_id=nearby[-by],
+                device_id_type=MESH,
+            )
+        )
+        sum_copies[-1].start()
+    halo[2].wait_recv()
+    halo[3].wait_recv()
+    length_float = length.astype(jnp.float32)
+    for g in range(GROUPS):
+        column = jnp.concatenate([sums[block, 4 * g : 4 * g + 4] for block in range(3)], 1)
+        split = jnp.concatenate([column, jnp.zeros_like(column)], 0)
+        out = jnp.dot(two_halves(split), values[:, g * HD : (g + 1) * HD], preferred_element_type=jnp.float32)
+        pooled_ref[4 * g : 4 * g + 4] = (out[:4] + out[8:12]) / length_float
 
     pair = core_copy(pooled_ref.at[pl.ds((1 - core) * HALF, HALF)], core_buf, send.at[1], recv.at[1])
     pair.start()
@@ -256,7 +340,8 @@
     own_mean = jnp.sqrt(jnp.sum(jnp.sum(own * own, 1, keepdims=True), 0, keepdims=True) / 2048.0 + norm_eps)
     own_scale = own_mean * 2048.0**0.5
     emb = own / own_scale
-    emb_ref[...] = emb
+    for h in range(HEADS):
+        emb_ref[:, h * HD : (h + 1) * HD] = emb[h : h + 1]
     t_pair.wait_recv()
     t_full[pl.ds(core * HALF, HALF)] = t_own[pl.ds(0, HALF)]
     t_full[pl.ds((1 - core) * HALF, HALF)] = t_half[...]
@@ -300,8 +385,80 @@
         inverse_temp * loss_scale / DOCS * (ring_full[...] / student_total - t_sum / target_total)
     )
     inner = jnp.sum(jnp.sum(emb * unit_grad, 1, keepdims=True), 0, keepdims=True)
-    cot_ref[...] = (unit_grad - emb * inner) / own_scale / len_ref[0].astype(jnp.float32)
-
+    cot = (unit_grad - emb * inner) / own_scale / length_float
+    cot_wide = jnp.concatenate([cot] * GROUPS, 1)
+    mine_only = lax.broadcasted_iota(jnp.int32, (HEADS, GROUPS * HD), 1) // HD == (
+        lax.broadcasted_iota(jnp.int32, (HEADS, GROUPS * HD), 0) // 4
+    )
+    cot_diag = jnp.where(mine_only, cot_wide, 0.0).astype(jnp.bfloat16)
+    prob_grad = lax.dot_general(
+        cot_diag, values[...], (((1,), (1,)), ((), ())), preferred_element_type=jnp.float32
+    )
+
+    dk_copies = []
+    for g in range(GROUPS):
+        for j in range(4):
+            h = 4 * g + j
+            part = prob[h]
+            push = part * prob_grad[h : h + 1]
+            total = push[:, :BLOCK] + push[:, BLOCK : 2 * BLOCK] + push[:, 2 * BLOCK :]
+            score[g, j * BLOCK : (j + 1) * BLOCK] = (push - part * jnp.sum(total, 1, keepdims=True)).astype(
+                jnp.bfloat16
+            )
+        for i, by in enumerate((1, 2)):
+            block = 2 - by
+            dk_out[i, g] = (
+                lax.dot_general(
+                    score[g, :, block * BLOCK : (block + 1) * BLOCK],
+                    stacked(g),
+                    (((0,), (0,)), ((), ())),
+                    preferred_element_type=jnp.float32,
+                )
+                * HD ** (-0.5)
+            ).astype(dk_out.dtype)
+            copy = pltpu.make_async_remote_copy(
+                src_ref=dk_out.at[i, g],
+                dst_ref=dk_in.at[i, g],
+                send_sem=near_send.at[6 + i],
+                recv_sem=near_recv.at[6 + i],
+                device_id=nearby[-by],
+                device_id_type=MESH,
+            )
+            copy.start()
+    for copy in sum_copies:
+        copy.wait_recv()
+    sums_all = sums[2] + sums_in[0] + sums_in[1]
+    high = sums_all.astype(jnp.bfloat16)
+    low = (sums_all - high.astype(jnp.float32)).astype(jnp.bfloat16)
+    dv_ref[0] = lax.dot_general(
+        jnp.concatenate([high, low], 0),
+        jnp.concatenate([cot_diag, cot_diag], 0),
+        (((0,), (0,)), ((), ())),
+        preferred_element_type=jnp.float32,
+    ).astype(jnp.bfloat16)
+    dk_own = []
+    for g in range(GROUPS):
+        dq = jnp.dot(score[g], keys[:, g * HD : (g + 1) * HD], preferred_element_type=jnp.float32) * HD ** (-0.5)
+        for j in range(4):
+            h = 4 * g + j
+            dq_ref[0, :, h * HD : (h + 1) * HD] = dq[j * BLOCK : (j + 1) * BLOCK].astype(jnp.bfloat16)
+        dk_own.append(
+            lax.dot_general(
+                score[g, :, 2 * BLOCK :], stacked(g), (((0,), (0,)), ((), ())), preferred_element_type=jnp.float32
+            )
+            * HD ** (-0.5)
+        )
+    for i in range(2):
+        wait_bytes(dk_in.at[i], near_recv.at[6 + i])
+    for g in range(GROUPS):
+        dk_ref[0, :, g * HD : (g + 1) * HD] = (
+            dk_own[g] + dk_in[0, g].astype(jnp.float32) + dk_in[1, g].astype(jnp.float32)
+        ).astype(jnp.bfloat16)
+
+    for copy in halo + sum_copies:
+        copy.wait_send()
+    for i in range(2):
+        wait_bytes(dk_out.at[i], near_send.at[6 + i])
     wait_bytes(tp.at[pl.ds(0, PLANE - 1), pl.ds(0, ROWS)], send.at[0])
     pair.wait_send()
     wait_bytes(zb.at[pl.ds(0, NZ - 1)], send.at[2])
@@ -313,22 +470,42 @@
     e_pair.wait_send()
 
 
-def queue_part(pooled, lengths, queue_keys, write_pos, teacher):
+def shards(query_states, key_states, value_states, lengths, queue_keys, write_pos, teacher):
     vmem = pl.BlockSpec(memory_space=pltpu.VMEM)
     smem = pl.BlockSpec(memory_space=pltpu.SMEM)
-    f32 = lambda *shape: pltpu.VMEM(shape, jnp.float32)
-    return pl.pallas_call(
-        queue_kernel,
-        name="queue_part",
+    anywhere = pl.BlockSpec(memory_space=pl.ANY)
+
+    def f32(*shape):
+        return pltpu.VMEM(shape, jnp.float32)
+
+    def b16(*shape):
+        return pltpu.VMEM(shape, jnp.bfloat16)
+
+    loss, unit_vec, grad_query, grad_key, grad_value = pl.pallas_call(
+        whole_kernel,
+        name="whole",
         out_shape=(
-            jax.ShapeDtypeStruct((HEADS, HD), jnp.float32),
-            jax.ShapeDtypeStruct((HEADS, HD), jnp.float32),
             jax.ShapeDtypeStruct((1, 1), jnp.float32),
+            jax.ShapeDtypeStruct((1, HEADS * HD), jnp.float32),
+            jax.ShapeDtypeStruct(query_states.shape, jnp.bfloat16),
+            jax.ShapeDtypeStruct(key_states.shape, jnp.bfloat16),
+            jax.ShapeDtypeStruct(value_states.shape, jnp.bfloat16),
         ),
-        in_specs=[smem, smem, vmem, pl.BlockSpec(memory_space=pl.ANY), vmem],
-        out_specs=(vmem, vmem, vmem),
+        in_specs=[smem, smem] + [anywhere] * 5,
+        out_specs=(vmem,) * 5,
         scratch_shapes=[
-            pltpu.VMEM((EXT, 2048), jnp.bfloat16),
+            b16(BLOCK, HEADS * HD),
+            b16(3 * BLOCK, GROUPS * HD),
+            b16(3 * BLOCK, GROUPS * HD),
+            f32(DOCS, ENTRIES),
+            f32(HEADS, BLOCK, 3 * BLOCK),
+            f32(3, HEADS, BLOCK),
+            f32(2, HEADS, BLOCK),
+            b16(2, GROUPS, BLOCK, HD),
+            b16(2, GROUPS, BLOCK, HD),
+            b16(GROUPS, 4 * BLOCK, 3 * BLOCK),
+            f32(HEADS, HD),
+            b16(EXT, 2048),
             f32(16, 128),
             f32(HALF, 128),
             f32(NZ, HALF, 128),
@@ -349,108 +526,17 @@
             f32(DOCS, HEADS, 128),
             f32(16, 128),
             pltpu.SemaphoreType.REGULAR,
-            pltpu.SemaphoreType.DMA,
+            pltpu.SemaphoreType.DMA((5,)),
             pltpu.SemaphoreType.DMA((9,)),
             pltpu.SemaphoreType.DMA((9,)),
+            pltpu.SemaphoreType.DMA((8,)),
+            pltpu.SemaphoreType.DMA((8,)),
         ],
         compiler_params=pltpu.CompilerParams(
-            collective_id=0, has_side_effects=True, vmem_limit_bytes=32 * 1024 * 1024
+            collective_id=0, has_side_effects=True, vmem_limit_bytes=40 * 1024 * 1024
         ),
-    )(write_pos, lengths, pooled, queue_keys, teacher)
-
-
-def shards(query_states, key_states, value_states, lengths, queue_keys, write_pos, teacher):
-    docs_here, row_count, width = query_states.shape
-    kv_width = key_states.shape[2]
-    heads_kv = kv_width // HD
-    grouped = query_states.reshape(docs_here, row_count, heads_kv, -1, HD)
-    score_scale = HD ** (-0.5)
-    ctx_index = lax.axis_index("ctx")
-    query_pos = ctx_index * row_count + jnp.arange(row_count, dtype=jnp.int32)
-    window_rows = SPAN * row_count
-    kv_pair = jnp.stack((key_states, value_states))
-    kv_blocks = [kv_pair]
-    moving = kv_pair
-    for offset in range(SPAN):
-        moving = from_behind(moving, "ctx", 1)
-        kv_blocks.append(moving)
-    weights = []
-    denominator = 0.0
-    numerator = 0.0
-    for offset in range(SPAN + 1):
-        key_tile = kv_blocks[offset][0].reshape(docs_here, row_count, heads_kv, HD)
-        value_tile = kv_blocks[offset][1].reshape(docs_here, row_count, heads_kv, HD)
-        key_pos = (ctx_index - offset) * row_count + jnp.arange(row_count, dtype=jnp.int32)
-        visible = (
-            (key_pos[None, :] <= query_pos[:, None])
-            & (key_pos[None, :] > query_pos[:, None] - window_rows)
-            & (key_pos[None, :] >= 0)
-        )
-        scores = (
-            jnp.einsum("dqkgh,dtkh->dkgqt", grouped, key_tile, preferred_element_type=jnp.float32)
-            * score_scale
-        )
-        weight = jnp.where(visible, jnp.exp(scores), 0.0)
-        weights.append(weight)
-        denominator = denominator + jnp.sum(weight, -1)
-        numerator = numerator + jnp.einsum(
-            "dkgqt,dtkh->dkgqh",
-            weight.astype(jnp.bfloat16),
-            value_tile,
-            preferred_element_type=jnp.float32,
-        )
-    output = numerator / denominator[..., None]
-    live_rows = (query_pos[None, :] < lengths[:, None])[:, None, None, :, None]
-    length_float = lengths[:, None].astype(jnp.float32)
-    pooled = jnp.sum(jnp.where(live_rows, output, 0.0), 3).reshape(docs_here, -1) / length_float
-    emb, cot, loss = queue_part(
-        pooled.reshape(HEADS, HD), lengths, queue_keys, write_pos, teacher
-    )
-    unit_vec = emb.reshape(docs_here, width)
-    loss_value = loss[0, 0]
-    cotangent = cot.reshape(docs_here, heads_kv, -1, HD)
-    cot_round = cotangent.astype(jnp.bfloat16)
-    row_dot = jnp.sum(cotangent[:, :, :, None, :] * output, -1)
-    query_grad = 0.0
-    tile_grads = []
-    for offset in range(SPAN + 1):
-        key_tile = kv_blocks[offset][0].reshape(docs_here, row_count, heads_kv, HD)
-        value_tile = kv_blocks[offset][1].reshape(docs_here, row_count, heads_kv, HD)
-        attn_prob = jnp.where(live_rows, weights[offset] / denominator[..., None], 0.0)
-        prob_grad = jnp.einsum(
-            "dkgh,dtkh->dkgt", cot_round, value_tile, preferred_element_type=jnp.float32
-        )
-        score_grad = attn_prob * (prob_grad[:, :, :, None, :] - row_dot[..., None])
-        score_round = score_grad.astype(jnp.bfloat16)
-        query_grad = query_grad + jnp.einsum(
-            "dkgqt,dtkh->dqkgh", score_round, key_tile, preferred_element_type=jnp.float32
-        )
-        key_part = (
-            jnp.einsum(
-                "dkgqt,dqkgh->dtkh", score_round, grouped, preferred_element_type=jnp.float32
-            )
-            * score_scale
-        )
-        value_part = jnp.einsum(
-            "dkgqt,dkgh->dtkh",
-            attn_prob.astype(jnp.bfloat16),
-            cot_round,
-            preferred_element_type=jnp.float32,
-        )
-        tile_grads.append(
-            jnp.stack((key_part, value_part)).reshape(2, docs_here, row_count, kv_width)
-        )
-    kv_grad = tile_grads[SPAN]
-    for offset in range(SPAN - 1, -1, -1):
-        kv_grad = from_behind(kv_grad, "ctx", -1) + tile_grads[offset]
-    query_out = (query_grad * score_scale).reshape(docs_here, row_count, width).astype(jnp.bfloat16)
-    return (
-        loss_value,
-        unit_vec,
-        query_out,
-        kv_grad[0].astype(jnp.bfloat16),
-        kv_grad[1].astype(jnp.bfloat16),
-    )
+    )(write_pos, lengths, query_states, key_states, value_states, queue_keys, teacher)
+    return loss[0, 0], unit_vec, grad_query, grad_key, grad_value
 
 
 def solution(mesh):

time: 110 us -> 75.4 us (0.69)
  the two profiles are of different devices: /device:TPU:6 before, /device:TPU:1 now
where the time goes in v2:
time: 75.4 us; the launch traced here: 75.1 us
  Pallas kernels  64.5 us (86%)
  local copies, waits for them, and re-layouts  7.47 us (10%)
  between operations  3.15 us (4%)
    pallas_call x1, Pallas kernels, shards(): pl.pallas_call(whole_kernel, name='whole', out_shape=(jax.ShapeDtypeStruc...  64.5 us
    unnamed x16, local copies, waits for them, and re-layouts  7.47 us

profile of v2, /device:TPU:1, one launch (start us, length us, event | category | flops | bytes accessed | tf_op | source)
XLA Modules:
  0.0 75.1 jit_solution(9646331081179010622)
XLA Ops:
  0.6 0.0 copy-start.5
  1.3 0.0 copy-done.5
  1.3 0.0 copy-start
  1.3 1.2 %copy-done = bf16[256,2048]{1,0:T(8,128)(2,1)S(1)} copy-done((bf16[256,2048]{1,0:T(8,128)(2,1)S(1)}, bf16[256,2048]{1,0:T(8,128)(2,1)}, u32[]{:S(2)}) %copy-start) | copy-done | bytes 1048600
  2.5 0.0 copy-start.1
  2.5 1.0 %copy-done.1 = bf16[1,128,2048]{2,1,0:T(8,128)(2,1)S(1)} copy-done((bf16[1,128,2048]{2,1,0:T(8,128)(2,1)S(1)}, bf16[1,128,2048]{2,1,0:T(8,128)(2,1)}, u32[]{:S(2)}) %copy-start.1) | copy-done | bytes 524312
  3.6 0.0 copy-start.2
  3.6 0.9 %copy-done.2 = bf16[1,128,512]{2,1,0:T(8,128)(2,1)S(1)} copy-done((bf16[1,128,512]{2,1,0:T(8,128)(2,1)S(1)}, bf16[1,128,512]{2,1,0:T(8,128)(2,1)}, u32[]{:S(2)}) %copy-start.2) | copy-done | bytes 131096
  4.5 0.0 copy-start.3
  4.5 0.9 %copy-done.3 = bf16[1,128,512]{2,1,0:T(8,128)(2,1)S(1)} copy-done((bf16[1,128,512]{2,1,0:T(8,128)(2,1)S(1)}, bf16[1,128,512]{2,1,0:T(8,128)(2,1)}, u32[]{:S(2)}) %copy-start.3) | copy-done | bytes 131096
  5.4 0.0 copy-start.4
  5.4 0.7 copy-done.4
  6.1 64.5 %whole.1 = (f32[1,1]{1,0:T(1,128)}, f32[1,2048]{1,0:T(1,128)S(1)}, bf16[1,128,2048]{2,1,0:T(8,128)(2,1)S(1)}, bf16[1,128,512]{2,1,0:T(8,128)(2,1)S(1)}, bf16[1,128,512]{2,1,0:T(8,128)(2,1)S(1)}) custom-call(s32[8]{0:T(128)S(1)} %copy-done.5, s32[1]{0:T(128)S(6)} %copy.17.len_ref, bf16[1,128,2048]{2,1,0:T(8,128)(2,1)S(1)} %copy-done.1, ...), custom_call_target="tpu_custom_call" | custom-call | tf_op jit(solution)/shard_map/whole/pallas_call | solution.py:484
  71.3 0.6 copy.19
  71.9 0.8 %copy.20 = bf16[1,128,2048]{2,1,0:T(8,128)(2,1)} copy(bf16[1,128,2048]{2,1,0:T(8,128)(2,1)S(1)} %get-tuple-element.22) | data formatting | bytes 1048576
  72.7 0.7 copy.21
  73.3 0.7 copy.22
Async XLA Ops:
  0.6 0.7 copy-start.5
  1.3 1.2 %copy-start = (bf16[256,2048]{1,0:T(8,128)(2,1)S(1)}, bf16[256,2048]{1,0:T(8,128)(2,1)}, u32[]{:S(2)}) copy-start(bf16[256,2048]{1,0:T(8,128)(2,1)} %queue_ref.1) | copy-start | bytes 3145732
  2.5 1.0 %copy-start.1 = (bf16[1,128,2048]{2,1,0:T(8,128)(2,1)S(1)}, bf16[1,128,2048]{2,1,0:T(8,128)(2,1)}, u32[]{:S(2)}) copy-start(bf16[1,128,2048]{2,1,0:T(8,128)(2,1)} %query_hbm.1) | copy-start | bytes 1572868
  3.6 0.9 %copy-start.2 = (bf16[1,128,512]{2,1,0:T(8,128)(2,1)S(1)}, bf16[1,128,512]{2,1,0:T(8,128)(2,1)}, u32[]{:S(2)}) copy-start(bf16[1,128,512]{2,1,0:T(8,128)(2,1)} %key_hbm.1) | copy-start | bytes 393220
  4.5 0.9 %copy-start.3 = (bf16[1,128,512]{2,1,0:T(8,128)(2,1)S(1)}, bf16[1,128,512]{2,1,0:T(8,128)(2,1)}, u32[]{:S(2)}) copy-start(bf16[1,128,512]{2,1,0:T(8,128)(2,1)} %value_hbm.1) | copy-start | bytes 393220
  5.4 0.7 copy-start.4

commit v3 on v1

v3 whole, which is shorter than its diff:
```python
import functools

import jax
import jax.numpy as jnp
from jax import lax
from jax.experimental import pallas as pl
from jax.experimental.pallas import tpu as pltpu
from jax.sharding import PartitionSpec as P

HD = 128
HEADS = 16
GROUPS = 2
BLOCK = 128
KV = GROUPS * HD
CHIPS = 32
HALF = 8
WIDE = HALF * HD
DOCS = 8
ENTRIES = 256
EXT = ENTRIES + 128
NZ = 16
PLANE = 32
T_ROWS = 10
ROWS = 11

inverse_temp = 10.0
loss_scale = 2.0**24
norm_eps = 1e-06

MESH = pl.DeviceIdType.MESH


def position():
    ctx = lax.axis_index("ctx")
    grp = lax.axis_index("grp")
    return ctx // 32, (ctx // 2) % NZ, ctx % 2, grp


def device(x_hi, z, core, grp):
    return ((x_hi * NZ + z) * 2 + core, grp)


def shifted(dx=0, dy=0, dz=0, dc=0):
    x_hi, z, core, grp = position()
    x = (2 * x_hi + grp // 4 + dx) % 4
    return device(x // 2, (z + dz) % NZ, (core + dc) % 2, (x % 2) * 4 + (grp + dy) % 4)


def plane_peer(step):
    x_hi, z, core, grp = position()
    turn = (step // 4) % 4
    turn = turn + turn // 2 - 2 * (turn // 3)
    px = (x_hi + step // 16) % 2
    pc = (core + step % 2) % 2
    pl_x = (grp // 4 + (step // 2) % 2) % 2
    py = (grp + turn) % 4
    return px, pc, pl_x * 4 + py


def z_offset(step):
    return 8 + ((step + 1) // 2) * (2 * (step % 2) - 1)


def send_plane(src_of, dst, send_sem, recv_sem):
    x_hi, z, core, grp = position()
    mine = x_hi * 16 + core * 8 + grp

    def one(k, carry):
        px, pc, pg = plane_peer(31 - k)
        pltpu.make_async_remote_copy(
            src_ref=src_of(pc, pg),
            dst_ref=dst(mine),
            send_sem=send_sem,
            recv_sem=recv_sem,
            device_id=device(px, z, pc, pg),
            device_id_type=MESH,
        ).start()
        return carry

    lax.fori_loop(0, PLANE - 1, one, 0)


def send_ring(src, dst, send_sem, recv_sem):
    x_hi, z, core, grp = position()

    def one(k, carry):
        pltpu.make_async_remote_copy(
            src_ref=src,
            dst_ref=dst(z),
            send_sem=send_sem,
            recv_sem=recv_sem,
            device_id=device(x_hi, (z + z_offset(k)) % NZ, core, grp),
            device_id_type=MESH,
        ).start()
        return carry

    lax.fori_loop(0, NZ - 1, one, 0)


def wait_bytes(ref, sem):
    pltpu.make_async_copy(ref, ref, sem).wait()


def sum_slots(ref, count):
    total = ref[0]
    for i in range(1, count):
        total = total + ref[i]
    return total


def two_halves(x):
    high = x.astype(jnp.bfloat16).astype(jnp.float32)
    return jnp.concatenate([high, x - high], 0).astype(jnp.bfloat16)


def whole_kernel(
    pos_ref, len_ref, query_hbm, key_hbm, value_hbm, queue_ref, teacher_hbm,
    loss_ref, emb_ref, dq_ref, dk_ref, dv_ref,
    query_out, key_out, value_out, query, keys, values, teacher_ref, prob, sums, sums_in, score,
    dk_out, dk_in, dk_chip, dk_part, dv_chip, dv_part, dq_chip, dq_part,
    eff, mix, zb, pb, t_out, tp, tz, t_own, t_half, s_out, ep, ez, half_sum, ring_out,
    t_ring_out, t_full, unit_rows, e_ring_out,
    ready, load_sem, send, recv, near_send, near_recv,
):
    x_hi, z, core, grp = position()
    mine = x_hi * 16 + core * 8 + grp
    ctx = (x_hi * NZ + z) * 2 + core
    chip = x_hi * NZ + z
    twin = (chip * 2 + 1 - core, grp)

    def beside(by, which):
        return ((chip + CHIPS + by) % CHIPS * 2 + which, grp)

    barrier = pltpu.get_barrier_semaphore()
    first = [shifted(dx=dx, dy=dy) for dx in (1, 3) for dy in (1, 3)]
    first += [shifted(dz=2), shifted(dz=NZ - 2), shifted(dx=2), shifted(dy=2)]
    first += [beside(by, which) for by in (1, -1) for which in (0, 1)]
    first += [shifted(dz=1), shifted(dz=NZ - 1), shifted(dx=1), shifted(dx=3), shifted(dy=1), shifted(dy=3), twin]
    for to in first:
        pl.semaphore_signal(barrier, inc=1, device_id=to, device_id_type=MESH)

    loads = []
    for i, (source, goal) in enumerate((
        (key_hbm.at[0, :, pl.ds(0, KV)], key_out.at[0]),
        (key_hbm.at[0, :, pl.ds(KV, KV)], key_out.at[1]),
        (query_hbm.at[0, :, pl.ds(0, WIDE)], query_out.at[0]),
        (query_hbm.at[0, :, pl.ds(WIDE, WIDE)], query_out.at[1]),
        (value_hbm.at[0, :, pl.ds(0, KV)], value_out.at[0]),
        (value_hbm.at[0, :, pl.ds(KV, KV)], value_out.at[1]),
        (teacher_hbm, teacher_ref),
        (queue_ref, eff.at[pl.ds(0, ENTRIES)]),
        (key_hbm.at[0, :, pl.ds(pl.multiple_of(core * KV, KV), KV)], keys.at[2 + core]),
        (query_hbm.at[0, :, pl.ds(pl.multiple_of(core * WIDE, WIDE), WIDE)], query.at[core]),
        (value_hbm.at[0, :, pl.ds(pl.multiple_of(core * KV, KV), KV)], values.at[2 + core]),
    )):
        loads.append(pltpu.make_async_copy(source, goal, load_sem.at[i]))
        loads[-1].start()
    eff[pl.ds(ENTRIES, 128)] = jnp.zeros((128, 2048), jnp.bfloat16)

    for i in range(6):
        loads[i].wait()
    pl.semaphore_wait(barrier, len(first))

    def start(source, goal, which, to):
        copy = pltpu.make_async_remote_copy(
            src_ref=source,
            dst_ref=goal,
            send_sem=near_send.at[which],
            recv_sem=near_recv.at[which],
            device_id=to,
            device_id_type=MESH,
        )
        copy.start()
        return copy

    def to_next(source, goal, which):
        for half in range(2):
            pltpu.make_async_remote_copy(
                src_ref=source.at[half],
                dst_ref=goal.at[core],
                send_sem=near_send.at[which + half],
                recv_sem=near_recv.at[which + core],
                device_id=beside(1, half),
                device_id_type=MESH,
            ).start()

    to_next(key_out, keys, 0)
    start(key_out.at[1 - core], keys.at[2 + core], 2, twin)
    start(query_out.at[1 - core], query.at[core], 3, twin)
    start(value_out.at[1 - core], values.at[2 + core], 6, twin)
    to_next(value_out, values, 4)
    for to in (shifted(dz=2), shifted(dz=NZ - 2), shifted(dx=2), shifted(dy=2), twin):
        pl.semaphore_signal(ready.at[0], inc=1, device_id=to, device_id_type=MESH)

    base = (ctx * 8 + grp) * ENTRIES
    entry = lax.broadcasted_iota(jnp.int32, (DOCS, ENTRIES), 1) + base
    lane = lax.broadcasted_iota(jnp.int32, (DOCS, 128), 1)
    row = lax.broadcasted_iota(jnp.int32, (DOCS, 128), 0)
    loads[6].wait()
    teacher = teacher_ref[...]
    kept = jnp.ones((DOCS, ENTRIES), jnp.float32)
    there = jnp.zeros((DOCS, 128), jnp.float32)
    teacher_at = jnp.zeros((DOCS, 128), jnp.float32)
    for d in range(DOCS):
        hit = (entry == pos_ref[d]).astype(jnp.float32)
        kept = kept - hit
        at = (lane == d).astype(jnp.float32)
        there = there + at * jnp.sum(hit, 1, keepdims=True)
        teacher_at = teacher_at + at * jnp.sum(teacher * hit, 1, keepdims=True)
    target = jnp.where(kept > 0, jnp.exp(teacher), 0.0)
    target_at = jnp.where(there > 0, jnp.exp(teacher_at), 0.0)
    target_sum = jnp.sum(target, 1, keepdims=True) + jnp.sum(target_at, 1, keepdims=True)
    sum_row = jnp.sum(jnp.where(lane == row, target_sum, 0.0), 0, keepdims=True)

    def spread(out, part):
        for h in range(HEADS):
            out[:, h // HALF, h % HALF] = part[:, h * HD : (h + 1) * HD]

    loads[7].wait()
    mixed = jnp.dot(two_halves(target), eff[pl.ds(0, ENTRIES)], preferred_element_type=jnp.float32)
    spread(t_out, mixed[:DOCS] + mixed[DOCS:])
    for c in range(2):
        t_out[:, c, HALF] = target_at
        for d in range(DOCS):
            t_out[d, c, pl.ds(HALF + 1, 1)] = sum_row

    pl.semaphore_wait(ready.at[0], 5)
    pl.semaphore_signal(ready.at[1], inc=1, device_id=twin, device_id_type=MESH)
    for to in (4, NZ - 4):
        pl.semaphore_signal(ready.at[2], inc=1, device_id=shifted(dz=to), device_id_type=MESH)

    later = lax.broadcasted_iota(jnp.int32, (BLOCK, BLOCK), 1)
    rows = lax.broadcasted_iota(jnp.int32, (BLOCK, BLOCK), 0)
    inside = (later > rows, None, later <= rows)

    def stacked(r, g):
        return jnp.concatenate([query[r, :, (4 * g + j) * HD : (4 * g + j + 1) * HD] for j in range(4)], 0)

    def weigh(r, s):
        for g in range(GROUPS):
            tile = keys[r + s, :, g * HD : (g + 1) * HD]
            scores = lax.dot_general(
                stacked(r, g), tile, (((1,), (1,)), ((), ())), preferred_element_type=jnp.float32
            )
            weight = jnp.exp(scores * HD ** (-0.5)).reshape(4, BLOCK, BLOCK)
            seen = inside[s]
            if r + s < 2:
                before = jnp.broadcast_to(chip >= 1, (BLOCK, BLOCK))
                seen = before if seen is None else seen & before
            if seen is not None:
                weight = jnp.where(seen[None], weight, 0.0)
            prob[r, 4 * g : 4 * g + 4, :, s * BLOCK : (s + 1) * BLOCK] = weight

    def arrived(ref, which):
        wait_bytes(ref, near_recv.at[which])

    for i in (8, 9, 10):
        loads[i].wait()
    arrived(key_out.at[0], 2)
    arrived(query_out.at[0], 3)
    weigh(0, 2)
    weigh(1, 1)
    weigh(1, 2)
    arrived(key_out.at[0], 0)
    arrived(key_out.at[0], 1)
    weigh(0, 0)
    weigh(0, 1)
    weigh(1, 0)

    length = len_ref[0]
    column = []
    for r in range(2):
        place = lax.broadcasted_iota(jnp.int32, (BLOCK, 1), 0) + (chip * 2 + r) * BLOCK
        live = (place < length).astype(jnp.float32)
        for h in range(HALF):
            weight = prob[r, h]
            total = weight[:, :BLOCK] + weight[:, BLOCK : 2 * BLOCK] + weight[:, 2 * BLOCK :]
            part = weight * (live / jnp.sum(total, 1, keepdims=True))
            prob[r, h] = part
            column.append(jnp.sum(part, 0, keepdims=True))
    for block in range(4):
        parts = []
        for r in range(2):
            s = block - r
            if 0 <= s < 3:
                parts.append(
                    jnp.concatenate([column[r * HALF + h][:, s * BLOCK : (s + 1) * BLOCK] for h in range(HALF)], 0)
                )
        sums[block] = parts[0] if len(parts) == 1 else parts[0] + parts[1]
    start(sums.at[pl.ds(0, 2)], sums_in, 7, beside(-1, core))

    pl.semaphore_wait(ready.at[1], 1)
    send_plane(
        lambda pc, pg: t_out.at[pg, pc, pl.ds(0, T_ROWS)],
        lambda me: tp.at[me, pl.ds(0, T_ROWS)],
        send.at[0],
        recv.at[0],
    )
    tp[mine] = t_out[grp, core]

    arrived(value_out.at[0], 6)
    arrived(sums_in, 7)
    length_float = length.astype(jnp.float32)
    sums_all = sums[pl.ds(2, 2)] + sums_in[...]
    for g in range(GROUPS):
        both = jnp.concatenate([sums_all[b, 4 * g : 4 * g + 4] for b in range(2)], 1)
        split = jnp.concatenate([both, jnp.zeros_like(both)], 0)
        tile = values[pl.ds(2, 2), :, g * HD : (g + 1) * HD].reshape(2 * BLOCK, HD)
        out = jnp.dot(two_halves(split), tile, preferred_element_type=jnp.float32)
        half_sum[4 * g : 4 * g + 4] = (out[:4] + out[8:12]) / length_float

    pl.semaphore_wait(ready.at[2], 2)
    send_ring(half_sum, lambda me: zb.at[me], send.at[2], recv.at[2])
    zb[z] = half_sum[...]

    wait_bytes(tp.at[pl.ds(0, PLANE - 1), pl.ds(0, T_ROWS)], recv.at[0])
    t_ring_out[...] = sum_slots(tp, PLANE)
    send_ring(t_ring_out.at[pl.ds(0, T_ROWS)], lambda me: tz.at[me, pl.ds(0, T_ROWS)], send.at[3], recv.at[3])
    tz[z] = t_ring_out[...]

    wait_bytes(zb.at[pl.ds(0, NZ - 1)], recv.at[2])
    ring_out[...] = sum_slots(zb, NZ)
    send_plane(lambda pc, pg: ring_out, lambda me: pb.at[me], send.at[4], recv.at[4])
    pb[mine] = ring_out[...]

    wait_bytes(tz.at[pl.ds(0, NZ - 1), pl.ds(0, T_ROWS)], recv.at[3])
    t_own[...] = sum_slots(tz, NZ)
    t_pair = pltpu.make_async_remote_copy(
        src_ref=t_own.at[pl.ds(0, HALF)],
        dst_ref=t_half,
        send_sem=send.at[5],
        recv_sem=recv.at[5],
        device_id=twin,
        device_id_type=MESH,
    )
    t_pair.start()

    wait_bytes(pb.at[pl.ds(0, PLANE - 1)], recv.at[4])
    heads = []
    for c in range(2):
        both = pb[pl.ds(c * 8, 8)] + pb[pl.ds(16 + c * 8, 8)]
        unit_rows[:, pl.ds(c * HALF, HALF)] = both
    square = jnp.zeros((DOCS, HD), jnp.float32)
    for h in range(HEADS):
        tile = unit_rows[:, h]
        heads.append(tile)
        square = square + tile * tile
    root_mean = jnp.sqrt(jnp.sum(square, 1, keepdims=True) / 2048.0 + norm_eps)
    norm_scale = root_mean * 2048.0**0.5
    for h in range(HEADS):
        unit = (heads[h] / norm_scale).astype(jnp.bfloat16)
        eff[pl.ds(ENTRIES, 16), h * HD : (h + 1) * HD] = jnp.concatenate([unit, jnp.zeros_like(unit)], 0)
    unit16 = eff[pl.ds(ENTRIES, 16)]
    logits = (
        lax.dot_general(unit16, eff[...], (((1,), (1,)), ((), ())), preferred_element_type=jnp.float32)[:DOCS]
        * inverse_temp
    )
    near, far = logits[:, :ENTRIES], logits[:, ENTRIES:]
    student = jnp.where(kept > 0, jnp.exp(near), 0.0)
    student_at = jnp.where(there > 0, jnp.exp(far), 0.0)
    student_sum = jnp.sum(student, 1, keepdims=True) + jnp.sum(student_at, 1, keepdims=True)
    cross = jnp.sum(target * (teacher - near), 1, keepdims=True) + jnp.sum(
        target_at * (teacher_at - far), 1, keepdims=True
    )
    student_row = jnp.sum(jnp.where(lane == row, student_sum, 0.0), 0, keepdims=True)
    cross_row = jnp.sum(jnp.where(lane == row, cross, 0.0), 0, keepdims=True)
    inner = jnp.sum(student * near, 1, keepdims=True) + jnp.sum(student_at * far, 1, keepdims=True)
    inner_row = jnp.sum(jnp.where(lane == row, inner, 0.0), 0, keepdims=True)
    mixed = jnp.dot(
        two_halves(jnp.concatenate([student, student_at], 1)), eff[...], preferred_element_type=jnp.float32
    )
    spread(s_out, mixed[:DOCS] + mixed[DOCS:])
    extra = jnp.concatenate([student_row, cross_row, inner_row], 0)
    for c in range(2):
        for d in range(DOCS):
            s_out[d, c, pl.ds(HALF, 3)] = extra
    send_plane(
        lambda pc, pg: s_out.at[pg, pc, pl.ds(0, ROWS)], lambda me: ep.at[me, pl.ds(0, ROWS)], send.at[6], recv.at[6]
    )
    ep[mine] = s_out[grp, core]

    own = unit_rows[grp]
    own_mean = jnp.sqrt(jnp.sum(jnp.sum(own * own, 1, keepdims=True), 0, keepdims=True) / 2048.0 + norm_eps)
    own_scale = own_mean * 2048.0**0.5
    emb = own / own_scale
    for h in range(HEADS):
        emb_ref[:, h * HD : (h + 1) * HD] = emb[h : h + 1]
    emb_half = unit_rows[grp, pl.ds(pl.multiple_of(core * HALF, HALF), HALF)] / own_scale
    t_pair.wait_recv()
    t_full[pl.ds(pl.multiple_of(core * HALF, HALF), HALF)] = t_own[pl.ds(0, HALF)]
    t_full[pl.ds(pl.multiple_of((1 - core) * HALF, HALF), HALF)] = t_half[...]
    t_sum = t_full[...]
    lane1 = lax.broadcasted_iota(jnp.int32, (1, 128), 1)
    at_row = t_own[pl.ds(HALF, 1)]
    target_row = t_own[pl.ds(HALF + 1, 1)]
    for d in range(DOCS):
        weight = jnp.sum(jnp.where(lane1 == d, at_row, 0.0), 1, keepdims=True)
        other = unit_rows[d]
        other_mean = jnp.sqrt(jnp.sum(jnp.sum(other * other, 1, keepdims=True), 0, keepdims=True) / 2048.0 + norm_eps)
        other_unit = (other / (other_mean * 2048.0**0.5)).astype(jnp.bfloat16).astype(jnp.float32)
        t_sum = t_sum + weight * other_unit
    target_total = jnp.sum(jnp.where(lane1 == grp, target_row, 0.0), 1, keepdims=True)
    unit_own = emb.astype(jnp.bfloat16).astype(jnp.float32)
    t_inner = jnp.sum(jnp.sum(unit_own * t_sum, 1, keepdims=True), 0, keepdims=True) / target_total
    t_full[...] = t_sum
    t_mean = t_full[pl.ds(pl.multiple_of(core * HALF, HALF), HALF)] / target_total
    mine_only = lax.broadcasted_iota(jnp.int32, (HALF, KV), 1) // HD == (
        lax.broadcasted_iota(jnp.int32, (HALF, KV), 0) // 4
    )
    arrived(value_out.at[0], 4)
    arrived(value_out.at[0], 5)

    wait_bytes(ep.at[pl.ds(0, PLANE - 1), pl.ds(0, ROWS)], recv.at[6])
    e_ring_out[...] = sum_slots(ep, PLANE)
    send_ring(e_ring_out.at[pl.ds(0, ROWS)], lambda me: ez.at[me, pl.ds(0, ROWS)], send.at[7], recv.at[7])
    ez[z] = e_ring_out[...]
    wait_bytes(ez.at[pl.ds(0, NZ - 1), pl.ds(0, ROWS)], recv.at[7])
    mix[...] = sum_slots(ez, NZ)
    student_all = mix[pl.ds(HALF, 1)]
    cross_all = mix[pl.ds(HALF + 1, 1)]
    student_total = jnp.sum(jnp.where(lane1 == grp, student_all, 0.0), 1, keepdims=True)
    s_inner = jnp.sum(jnp.where(lane1 == grp, mix[pl.ds(HALF + 2, 1)], 0.0), 1, keepdims=True) / (
        inverse_temp * student_total
    )
    factor = inverse_temp * loss_scale / DOCS
    unit_grad = factor * (mix[pl.ds(0, HALF)] / student_total - t_mean)
    cot = (unit_grad - emb_half * (factor * (s_inner - t_inner))) / own_scale / length_float
    cot_diag = jnp.where(mine_only, jnp.concatenate([cot] * GROUPS, 1), 0.0)
    cot_diag = jnp.concatenate([cot_diag, jnp.zeros_like(cot_diag)], 0).astype(jnp.bfloat16)
    prob_grad = lax.dot_general(
        cot_diag, values[...].reshape(4 * BLOCK, KV), (((1,), (1,)), ((), ())), preferred_element_type=jnp.float32
    )

    def scored(r):
        for h in range(HALF):
            part = prob[r, h]
            push = part * prob_grad[h : h + 1, r * BLOCK : (r + 3) * BLOCK]
            total = push[:, :BLOCK] + push[:, BLOCK : 2 * BLOCK] + push[:, 2 * BLOCK :]
            score[r, h // 4, (h % 4) * BLOCK : (h % 4 + 1) * BLOCK] = (
                push - part * jnp.sum(total, 1, keepdims=True)
            ).astype(jnp.bfloat16)

    def key_grad(block, g):
        total = None
        for r in range(2):
            s = block - r
            if 0 <= s < 3:
                one = lax.dot_general(
                    score[r, g, :, s * BLOCK : (s + 1) * BLOCK],
                    stacked(r, g),
                    (((0,), (0,)), ((), ())),
                    preferred_element_type=jnp.float32,
                )
                total = one if total is None else total + one
        return total * HD ** (-0.5)

    def send_back(block):
        for g in range(GROUPS):
            dk_out[block, :, g * HD : (g + 1) * HD] = key_grad(block, g).astype(jnp.bfloat16)
        pltpu.make_async_remote_copy(
            src_ref=dk_out.at[block],
            dst_ref=dk_in.at[core],
            send_sem=near_send.at[8 + block],
            recv_sem=near_recv.at[8 + core],
            device_id=beside(-1, block),
            device_id_type=MESH,
        ).start()

    scored(0)
    send_back(0)
    scored(1)
    send_back(1)
    for r in range(2):
        for g in range(GROUPS):
            tile = keys[pl.ds(r, 3), :, g * HD : (g + 1) * HD].reshape(3 * BLOCK, HD)
            dq = jnp.dot(score[r, g], tile, preferred_element_type=jnp.float32) * HD ** (-0.5)
            for j in range(4):
                h = 4 * g + j
                dq_chip[r, :, h * HD : (h + 1) * HD] = dq[j * BLOCK : (j + 1) * BLOCK].astype(jnp.bfloat16)
    start(dq_chip.at[1 - core], dq_part.at[core], 10, twin)
    for block in range(2):
        for g in range(GROUPS):
            dk_chip[block, :, g * HD : (g + 1) * HD] = key_grad(2 + block, g)
    start(dk_chip.at[1 - core], dk_part.at[core], 11, twin)
    for block in range(2):
        high = sums_all[block].astype(jnp.bfloat16).astype(jnp.float32)
        dv_chip[block] = lax.dot_general(
            jnp.concatenate([high, sums_all[block] - high], 0).astype(jnp.bfloat16),
            jnp.concatenate([cot_diag[:HALF], cot_diag[:HALF]], 0),
            (((0,), (0,)), ((), ())),
            preferred_element_type=jnp.float32,
        ).astype(jnp.bfloat16)
    start(dv_chip.at[1 - core], dv_part.at[core], 12, twin)
    dq_part[core] = dq_chip[core]
    dk_part[core] = dk_chip[core]
    dv_part[core] = dv_chip[core]
    terms = jnp.where(
        lane1 < DOCS,
        cross_all / jnp.where(lane1 < DOCS, target_row, 1.0)
        - jnp.log(jnp.where(lane1 < DOCS, target_row, 1.0))
        + jnp.log(jnp.where(lane1 < DOCS, student_all, 1.0)),
        0.0,
    )
    loss_ref[...] = jnp.sum(terms, 1, keepdims=True) / DOCS
    arrived(dq_chip.at[0], 10)
    for half in range(2):
        dq_ref[0, :, half * WIDE : (half + 1) * WIDE] = dq_part[half]
    arrived(dv_chip.at[0], 12)
    for half in range(2):
        dv_ref[0, :, half * KV : (half + 1) * KV] = dv_part[half]
    arrived(dk_chip.at[0], 11)
    for half in range(2):
        arrived(dk_out.at[0], 8 + half)
        dk_ref[0, :, half * KV : (half + 1) * KV] = (dk_part[half] + dk_in[half].astype(jnp.float32)).astype(
            jnp.bfloat16
        )

    for ref, which in (
        (key_out.at[0], 0), (key_out.at[0], 1), (key_out.at[0], 2), (query_out.at[0], 3), (value_out.at[0], 4),
        (value_out.at[0], 5), (value_out.at[0], 6), (sums_in, 7), (dk_out.at[0], 8), (dk_out.at[0], 9),
        (dq_chip.at[0], 10), (dk_chip.at[0], 11), (dv_chip.at[0], 12),
    ):
        wait_bytes(ref, near_send.at[which])
    wait_bytes(tp.at[pl.ds(0, PLANE - 1), pl.ds(0, T_ROWS)], send.at[0])
    wait_bytes(zb.at[pl.ds(0, NZ - 1)], send.at[2])
    wait_bytes(tz.at[pl.ds(0, NZ - 1), pl.ds(0, T_ROWS)], send.at[3])
    wait_bytes(pb.at[pl.ds(0, PLANE - 1)], send.at[4])
    t_pair.wait_send()
    wait_bytes(ep.at[pl.ds(0, PLANE - 1), pl.ds(0, ROWS)], send.at[6])
    wait_bytes(ez.at[pl.ds(0, NZ - 1), pl.ds(0, ROWS)], send.at[7])


def shards(query_states, key_states, value_states, lengths, queue_keys, write_pos, teacher):
    vmem = pl.BlockSpec(memory_space=pltpu.VMEM)
    smem = pl.BlockSpec(memory_space=pltpu.SMEM)
    anywhere = pl.BlockSpec(memory_space=pl.ANY)

    def f32(*shape):
        return pltpu.VMEM(shape, jnp.float32)

    def b16(*shape):
        return pltpu.VMEM(shape, jnp.bfloat16)

    loss, unit_vec, grad_query, grad_key, grad_value = pl.pallas_call(
        whole_kernel,
        name="whole",
        out_shape=(
            jax.ShapeDtypeStruct((1, 1), jnp.float32),
            jax.ShapeDtypeStruct((1, HEADS * HD), jnp.float32),
            jax.ShapeDtypeStruct(query_states.shape, jnp.bfloat16),
            jax.ShapeDtypeStruct(key_states.shape, jnp.bfloat16),
            jax.ShapeDtypeStruct(value_states.shape, jnp.bfloat16),
        ),
        in_specs=[smem, smem] + [anywhere] * 5,
        out_specs=(vmem,) * 5,
        scratch_shapes=[
            b16(2, BLOCK, WIDE),
            b16(2, BLOCK, KV),
            b16(2, BLOCK, KV),
            b16(2, BLOCK, WIDE),
            b16(4, BLOCK, KV),
            b16(4, BLOCK, KV),
            f32(DOCS, ENTRIES),
            f32(2, HALF, BLOCK, 3 * BLOCK),
            f32(4, HALF, BLOCK),
            f32(2, HALF, BLOCK),
            b16(2, GROUPS, 4 * BLOCK, 3 * BLOCK),
            b16(2, BLOCK, KV),
            b16(2, BLOCK, KV),
            f32(2, BLOCK, KV),
            f32(2, BLOCK, KV),
            b16(2, BLOCK, KV),
            b16(2, BLOCK, KV),
            b16(2, BLOCK, WIDE),
            b16(2, BLOCK, WIDE),
            b16(EXT, 2048),
            f32(16, 128),
            f32(NZ, HALF, 128),
            f32(PLANE, HALF, 128),
            f32(DOCS, 2, 16, 128),
            f32(PLANE, 16, 128),
            f32(NZ, 16, 128),
            f32(16, 128),
            f32(HALF, 128),
            f32(DOCS, 2, 16, 128),
            f32(PLANE, 16, 128),
            f32(NZ, 16, 128),
            f32(HALF, 128),
            f32(HALF, 128),
            f32(16, 128),
            f32(HEADS, 128),
            f32(DOCS, HEADS, 128),
            f32(16, 128),
            pltpu.SemaphoreType.REGULAR((3,)),
            pltpu.SemaphoreType.DMA((11,)),
            pltpu.SemaphoreType.DMA((8,)),
            pltpu.SemaphoreType.DMA((8,)),
            pltpu.SemaphoreType.DMA((13,)),
            pltpu.SemaphoreType.DMA((13,)),
        ],
        compiler_params=pltpu.CompilerParams(
            collective_id=0, has_side_effects=True, vmem_limit_bytes=56 * 1024 * 1024
        ),
    )(write_pos, lengths, query_states, key_states, value_states, queue_keys, teacher)
    return loss[0, 0], unit_vec, grad_query, grad_key, grad_value


def solution(mesh):
    placed = (
        P("grp", "ctx", None),
        P("grp", "ctx", None),
        P("grp", "ctx", None),
        P("grp"),
        P(("ctx", "grp"), None),
        P(),
        P(None, ("ctx", "grp")),
    )
    return jax.shard_map(
        shards,
        mesh=mesh,
        in_specs=placed,
        out_specs=(
            P(),
            P("grp", None),
            P("grp", "ctx", None),
            P("grp", "ctx", None),
            P("grp", "ctx", None),
        ),
        check_vma=False,
    )
```

time: 110 us -> 66.4 us (0.60)
  the two profiles are of different devices: /device:TPU:6 before, /device:TPU:1 now
where the time goes in v3:
time: 66.4 us; the launch traced here: 66.1 us
  Pallas kernels  58.9 us (89%)
  local copies, waits for them, and re-layouts  4.18 us (6%)
  between operations  3.06 us (5%)
    pallas_call x1, Pallas kernels, shards(): pl.pallas_call(whole_kernel, name='whole', out_shape=(jax.ShapeDtypeStruc...  58.9 us
    unnamed x10, local copies, waits for them, and re-layouts  4.18 us

profile of v3, /device:TPU:1, one launch (start us, length us, event | category | flops | bytes accessed | tf_op | source)
XLA Modules:
  0.0 66.1 jit_solution(18158097884436977764)
XLA Ops:
  1.3 58.9 %whole.1 = (f32[1,1]{1,0:T(1,128)}, f32[1,2048]{1,0:T(1,128)}, bf16[1,128,2048]{2,1,0:T(8,128)(2,1)}, bf16[1,128,512]{2,1,0:T(8,128)(2,1)}, bf16[1,128,512]{2,1,0:T(8,128)(2,1)}) custom-call(s32[8]{0:T(128)} %pos_ref.1, s32[1]{0:T(128)S(6)} %copy.17.len_ref, bf16[1,128,2048]{2,1,0:T(8,128)(2,1)} %query_hbm.1, bf16[1,128,512]{2,1,0:T(8,128)(2,1)} %key_hbm.1, ...), custom_call_target="tpu_custom_call" | custom-call | tf_op jit(solution)/shard_map/whole/pallas_call | solution.py:544
  60.2 0.0 copy-start.2
  60.8 0.1 copy-done.2
  60.9 0.6 copy.19
  61.5 0.0 copy-start.1
  61.5 1.9 %copy.20 = bf16[1,128,2048]{2,1,0:T(8,128)(2,1)} copy(bf16[1,128,2048]{2,1,0:T(8,128)(2,1)} %get-tuple-element.22) | data formatting | bytes 1048576
  63.4 0.0 copy-done.1
  63.4 0.0 copy-start
  63.4 0.7 copy.21
  64.0 0.3 copy-done
  64.3 0.7 copy.22
Async XLA Ops:
  60.2 0.7 %copy-start.2 = (f32[1,2048]{1,0:T(1,128)S(1)}, f32[1,2048]{1,0:T(1,128)}, u32[]{:S(2)}) copy-start(f32[1,2048]{1,0:T(1,128)} %get-tuple-element.21) | copy-start | bytes 24580
  61.5 1.9 %copy-start.1 = (bf16[1,128,512]{2,1,0:T(8,128)(2,1)S(1)}, bf16[1,128,512]{2,1,0:T(8,128)(2,1)}, u32[]{:S(2)}) copy-start(bf16[1,128,512]{2,1,0:T(8,128)(2,1)} %get-tuple-element.23) | copy-start | bytes 393220
  63.4 1.0 %copy-start = (bf16[1,128,512]{2,1,0:T(8,128)(2,1)S(1)}, bf16[1,128,512]{2,1,0:T(8,128)(2,1)}, u32[]{:S(2)}) copy-start(bf16[1,128,512]{2,1,0:T(8,128)(2,1)} %get-tuple-element.24) | copy-start | bytes 393220

commit v4 on v3

--- a/solution.py
+++ b/solution.py
@@ -17,11 +17,9 @@
 WIDE = HALF * HD
 DOCS = 8
 ENTRIES = 256
-EXT = ENTRIES + 128
 NZ = 16
 PLANE = 32
-T_ROWS = 10
-ROWS = 11
+ROWS = 9
 
 inverse_temp = 10.0
 loss_scale = 2.0**24
@@ -114,10 +112,10 @@
 
 
 def whole_kernel(
-    pos_ref, len_ref, query_hbm, key_hbm, value_hbm, queue_ref, teacher_hbm,
+    pos_hbm, len_hbm, query_hbm, key_hbm, value_hbm, queue_ref, teacher_hbm,
     loss_ref, emb_ref, dq_ref, dk_ref, dv_ref,
-    query_out, key_out, value_out, query, keys, values, teacher_ref, prob, sums, sums_in, score,
-    dk_out, dk_in, dk_chip, dk_part, dv_chip, dv_part, dq_chip, dq_part,
+    pos_ref, len_ref, query_out, key_out, value_out, query, keys, values, teacher_ref, prob, sums, sums_in, score,
+    dk_out, dk_in, dk_chip, dk_part, dv_chip, dq_chip,
     eff, mix, zb, pb, t_out, tp, tz, t_own, t_half, s_out, ep, ez, half_sum, ring_out,
     t_ring_out, t_full, unit_rows, e_ring_out,
     ready, load_sem, send, recv, near_send, near_recv,
@@ -148,14 +146,15 @@
         (value_hbm.at[0, :, pl.ds(0, KV)], value_out.at[0]),
         (value_hbm.at[0, :, pl.ds(KV, KV)], value_out.at[1]),
         (teacher_hbm, teacher_ref),
-        (queue_ref, eff.at[pl.ds(0, ENTRIES)]),
+        (queue_ref, eff),
         (key_hbm.at[0, :, pl.ds(pl.multiple_of(core * KV, KV), KV)], keys.at[2 + core]),
         (query_hbm.at[0, :, pl.ds(pl.multiple_of(core * WIDE, WIDE), WIDE)], query.at[core]),
         (value_hbm.at[0, :, pl.ds(pl.multiple_of(core * KV, KV), KV)], values.at[2 + core]),
+        (pos_hbm, pos_ref),
+        (len_hbm, len_ref),
     )):
         loads.append(pltpu.make_async_copy(source, goal, load_sem.at[i]))
         loads[-1].start()
-    eff[pl.ds(ENTRIES, 128)] = jnp.zeros((128, 2048), jnp.bfloat16)
 
     for i in range(6):
         loads[i].wait()
@@ -197,6 +196,8 @@
     lane = lax.broadcasted_iota(jnp.int32, (DOCS, 128), 1)
     row = lax.broadcasted_iota(jnp.int32, (DOCS, 128), 0)
     loads[6].wait()
+    loads[11].wait()
+    loads[12].wait()
     teacher = teacher_ref[...]
     kept = jnp.ones((DOCS, ENTRIES), jnp.float32)
     there = jnp.zeros((DOCS, 128), jnp.float32)
@@ -210,19 +211,17 @@
     target = jnp.where(kept > 0, jnp.exp(teacher), 0.0)
     target_at = jnp.where(there > 0, jnp.exp(teacher_at), 0.0)
     target_sum = jnp.sum(target, 1, keepdims=True) + jnp.sum(target_at, 1, keepdims=True)
-    sum_row = jnp.sum(jnp.where(lane == row, target_sum, 0.0), 0, keepdims=True)
+    target_row = jnp.sum(jnp.where(lane == row, target_sum, 0.0), 0, keepdims=True) + pltpu.roll(target_at, DOCS, 1)
 
     def spread(out, part):
         for h in range(HEADS):
             out[:, h // HALF, h % HALF] = part[:, h * HD : (h + 1) * HD]
 
     loads[7].wait()
-    mixed = jnp.dot(two_halves(target), eff[pl.ds(0, ENTRIES)], preferred_element_type=jnp.float32)
+    mixed = jnp.dot(two_halves(target), eff[...], preferred_element_type=jnp.float32)
     spread(t_out, mixed[:DOCS] + mixed[DOCS:])
     for c in range(2):
-        t_out[:, c, HALF] = target_at
-        for d in range(DOCS):
-            t_out[d, c, pl.ds(HALF + 1, 1)] = sum_row
+        t_out[:, c, HALF] = target_row
 
     pl.semaphore_wait(ready.at[0], 5)
     pl.semaphore_signal(ready.at[1], inc=1, device_id=twin, device_id_type=MESH)
@@ -291,8 +290,8 @@
 
     pl.semaphore_wait(ready.at[1], 1)
     send_plane(
-        lambda pc, pg: t_out.at[pg, pc, pl.ds(0, T_ROWS)],
-        lambda me: tp.at[me, pl.ds(0, T_ROWS)],
+        lambda pc, pg: t_out.at[pg, pc, pl.ds(0, ROWS)],
+        lambda me: tp.at[me, pl.ds(0, ROWS)],
         send.at[0],
         recv.at[0],
     )
@@ -313,27 +312,15 @@
     send_ring(half_sum, lambda me: zb.at[me], send.at[2], recv.at[2])
     zb[z] = half_sum[...]
 
-    wait_bytes(tp.at[pl.ds(0, PLANE - 1), pl.ds(0, T_ROWS)], recv.at[0])
+    wait_bytes(tp.at[pl.ds(0, PLANE - 1), pl.ds(0, ROWS)], recv.at[0])
     t_ring_out[...] = sum_slots(tp, PLANE)
-    send_ring(t_ring_out.at[pl.ds(0, T_ROWS)], lambda me: tz.at[me, pl.ds(0, T_ROWS)], send.at[3], recv.at[3])
-    tz[z] = t_ring_out[...]
 
     wait_bytes(zb.at[pl.ds(0, NZ - 1)], recv.at[2])
     ring_out[...] = sum_slots(zb, NZ)
     send_plane(lambda pc, pg: ring_out, lambda me: pb.at[me], send.at[4], recv.at[4])
     pb[mine] = ring_out[...]
-
-    wait_bytes(tz.at[pl.ds(0, NZ - 1), pl.ds(0, T_ROWS)], recv.at[3])
-    t_own[...] = sum_slots(tz, NZ)
-    t_pair = pltpu.make_async_remote_copy(
-        src_ref=t_own.at[pl.ds(0, HALF)],
-        dst_ref=t_half,
-        send_sem=send.at[5],
-        recv_sem=recv.at[5],
-        device_id=twin,
-        device_id_type=MESH,
-    )
-    t_pair.start()
+    send_ring(t_ring_out.at[pl.ds(0, ROWS)], lambda me: tz.at[me, pl.ds(0, ROWS)], send.at[3], recv.at[3])
+    tz[z] = t_ring_out[...]
 
     wait_bytes(pb.at[pl.ds(0, PLANE - 1)], recv.at[4])
     heads = []
@@ -347,37 +334,56 @@
         square = square + tile * tile
     root_mean = jnp.sqrt(jnp.sum(square, 1, keepdims=True) / 2048.0 + norm_eps)
     norm_scale = root_mean * 2048.0**0.5
-    for h in range(HEADS):
-        unit = (heads[h] / norm_scale).astype(jnp.bfloat16)
-        eff[pl.ds(ENTRIES, 16), h * HD : (h + 1) * HD] = jnp.concatenate([unit, jnp.zeros_like(unit)], 0)
-    unit16 = eff[pl.ds(ENTRIES, 16)]
-    logits = (
+    unit = [(heads[h] / norm_scale).astype(jnp.bfloat16) for h in range(HEADS)]
+    unit16 = jnp.concatenate(unit, 1)
+    unit16 = jnp.concatenate([unit16, jnp.zeros_like(unit16)], 0)
+    near = (
         lax.dot_general(unit16, eff[...], (((1,), (1,)), ((), ())), preferred_element_type=jnp.float32)[:DOCS]
         * inverse_temp
     )
-    near, far = logits[:, :ENTRIES], logits[:, ENTRIES:]
+    unit = [x.astype(jnp.float32) for x in unit]
+    far = jnp.zeros((DOCS, 128), jnp.float32)
+    for d in range(DOCS):
+        product = unit[0] * unit[0][d : d + 1]
+        for h in range(1, HEADS):
+            product = product + unit[h] * unit[h][d : d + 1]
+        far = far + jnp.where(lane == d, inverse_temp * jnp.sum(product, 1, keepdims=True), 0.0)
     student = jnp.where(kept > 0, jnp.exp(near), 0.0)
     student_at = jnp.where(there > 0, jnp.exp(far), 0.0)
     student_sum = jnp.sum(student, 1, keepdims=True) + jnp.sum(student_at, 1, keepdims=True)
     cross = jnp.sum(target * (teacher - near), 1, keepdims=True) + jnp.sum(
         target_at * (teacher_at - far), 1, keepdims=True
     )
-    student_row = jnp.sum(jnp.where(lane == row, student_sum, 0.0), 0, keepdims=True)
-    cross_row = jnp.sum(jnp.where(lane == row, cross, 0.0), 0, keepdims=True)
     inner = jnp.sum(student * near, 1, keepdims=True) + jnp.sum(student_at * far, 1, keepdims=True)
-    inner_row = jnp.sum(jnp.where(lane == row, inner, 0.0), 0, keepdims=True)
-    mixed = jnp.dot(
-        two_halves(jnp.concatenate([student, student_at], 1)), eff[...], preferred_element_type=jnp.float32
-    )
-    spread(s_out, mixed[:DOCS] + mixed[DOCS:])
-    extra = jnp.concatenate([student_row, cross_row, inner_row], 0)
+    extra = jnp.zeros((DOCS, 128), jnp.float32)
+    for i, value in enumerate((student_sum, cross, inner)):
+        extra = extra + jnp.where(lane == row + DOCS * i, value, 0.0)
+    extra = jnp.broadcast_to(jnp.sum(extra, 0, keepdims=True), (DOCS, 128))
+    mixed = jnp.dot(two_halves(student), eff[...], preferred_element_type=jnp.float32)
+    weights = [jnp.sum(jnp.where(lane == d, student_at, 0.0), 1, keepdims=True) for d in range(DOCS)]
+    for h in range(HEADS):
+        tile = mixed[:DOCS, h * HD : (h + 1) * HD] + mixed[DOCS:, h * HD : (h + 1) * HD]
+        for d in range(DOCS):
+            tile = tile + weights[d] * unit[h][d : d + 1]
+        s_out[:, h // HALF, h % HALF] = tile
     for c in range(2):
-        for d in range(DOCS):
-            s_out[d, c, pl.ds(HALF, 3)] = extra
+        s_out[:, c, HALF] = extra
     send_plane(
         lambda pc, pg: s_out.at[pg, pc, pl.ds(0, ROWS)], lambda me: ep.at[me, pl.ds(0, ROWS)], send.at[6], recv.at[6]
     )
     ep[mine] = s_out[grp, core]
+
+    wait_bytes(tz.at[pl.ds(0, NZ - 1), pl.ds(0, ROWS)], recv.at[3])
+    t_own[...] = sum_slots(tz, NZ)
+    t_pair = pltpu.make_async_remote_copy(
+        src_ref=t_own.at[pl.ds(0, HALF)],
+        dst_ref=t_half,
+        send_sem=send.at[5],
+        recv_sem=recv.at[5],
+        device_id=twin,
+        device_id_type=MESH,
+    )
+    t_pair.start()
 
     own = unit_rows[grp]
     own_mean = jnp.sqrt(jnp.sum(jnp.sum(own * own, 1, keepdims=True), 0, keepdims=True) / 2048.0 + norm_eps)
@@ -391,10 +397,9 @@
     t_full[pl.ds(pl.multiple_of((1 - core) * HALF, HALF), HALF)] = t_half[...]
     t_sum = t_full[...]
     lane1 = lax.broadcasted_iota(jnp.int32, (1, 128), 1)
-    at_row = t_own[pl.ds(HALF, 1)]
-    target_row = t_own[pl.ds(HALF + 1, 1)]
+    target_row = t_own[pl.ds(HALF, 1)]
     for d in range(DOCS):
-        weight = jnp.sum(jnp.where(lane1 == d, at_row, 0.0), 1, keepdims=True)
+        weight = jnp.sum(jnp.where(lane1 == DOCS + d, target_row, 0.0), 1, keepdims=True)
         other = unit_rows[d]
         other_mean = jnp.sqrt(jnp.sum(jnp.sum(other * other, 1, keepdims=True), 0, keepdims=True) / 2048.0 + norm_eps)
         other_unit = (other / (other_mean * 2048.0**0.5)).astype(jnp.bfloat16).astype(jnp.float32)
@@ -417,9 +422,9 @@
     wait_bytes(ez.at[pl.ds(0, NZ - 1), pl.ds(0, ROWS)], recv.at[7])
     mix[...] = sum_slots(ez, NZ)
     student_all = mix[pl.ds(HALF, 1)]
-    cross_all = mix[pl.ds(HALF + 1, 1)]
+    cross_all = pltpu.roll(student_all, 128 - DOCS, 1)
     student_total = jnp.sum(jnp.where(lane1 == grp, student_all, 0.0), 1, keepdims=True)
-    s_inner = jnp.sum(jnp.where(lane1 == grp, mix[pl.ds(HALF + 2, 1)], 0.0), 1, keepdims=True) / (
+    s_inner = jnp.sum(jnp.where(lane1 == grp + 2 * DOCS, student_all, 0.0), 1, keepdims=True) / (
         inverse_temp * student_total
     )
     factor = inverse_temp * loss_scale / DOCS
@@ -466,18 +471,22 @@
             device_id_type=MESH,
         ).start()
 
-    scored(0)
-    send_back(0)
-    scored(1)
-    send_back(1)
-    for r in range(2):
+    def query_grad(r):
         for g in range(GROUPS):
             tile = keys[pl.ds(r, 3), :, g * HD : (g + 1) * HD].reshape(3 * BLOCK, HD)
             dq = jnp.dot(score[r, g], tile, preferred_element_type=jnp.float32) * HD ** (-0.5)
             for j in range(4):
                 h = 4 * g + j
                 dq_chip[r, :, h * HD : (h + 1) * HD] = dq[j * BLOCK : (j + 1) * BLOCK].astype(jnp.bfloat16)
-    start(dq_chip.at[1 - core], dq_part.at[core], 10, twin)
+
+    scored(0)
+    send_back(0)
+    scored(1)
+    send_back(1)
+    own_wide = pl.ds(pl.multiple_of(core * WIDE, WIDE), WIDE)
+    own_kv = pl.ds(pl.multiple_of(core * KV, KV), KV)
+    query_grad(1 - core)
+    start(dq_chip.at[1 - core], dq_ref.at[0, :, own_wide], 10, twin)
     for block in range(2):
         for g in range(GROUPS):
             dk_chip[block, :, g * HD : (g + 1) * HD] = key_grad(2 + block, g)
@@ -490,10 +499,15 @@
             (((0,), (0,)), ((), ())),
             preferred_element_type=jnp.float32,
         ).astype(jnp.bfloat16)
-    start(dv_chip.at[1 - core], dv_part.at[core], 12, twin)
-    dq_part[core] = dq_chip[core]
+    start(dv_chip.at[1 - core], dv_ref.at[0, :, own_kv], 12, twin)
+    query_grad(core)
+    stays = [
+        pltpu.make_async_copy(dq_chip.at[core], dq_ref.at[0, :, own_wide], load_sem.at[0]),
+        pltpu.make_async_copy(dv_chip.at[core], dv_ref.at[0, :, own_kv], load_sem.at[1]),
+    ]
+    for copy in stays:
+        copy.start()
     dk_part[core] = dk_chip[core]
-    dv_part[core] = dv_chip[core]
     terms = jnp.where(
         lane1 < DOCS,
         cross_all / jnp.where(lane1 < DOCS, target_row, 1.0)
@@ -501,13 +515,7 @@
         + jnp.log(jnp.where(lane1 < DOCS, student_all, 1.0)),
         0.0,
     )
-    loss_ref[...] = jnp.sum(terms, 1, keepdims=True) / DOCS
-    arrived(dq_chip.at[0], 10)
-    for half in range(2):
-        dq_ref[0, :, half * WIDE : (half + 1) * WIDE] = dq_part[half]
-    arrived(dv_chip.at[0], 12)
-    for half in range(2):
-        dv_ref[0, :, half * KV : (half + 1) * KV] = dv_part[half]
+    loss_ref[...] = jnp.broadcast_to(jnp.sum(terms, 1, keepdims=True) / DOCS, (1, 128))
     arrived(dk_chip.at[0], 11)
     for half in range(2):
         arrived(dk_out.at[0], 8 + half)
@@ -515,24 +523,52 @@
             jnp.bfloat16
         )
 
+    arrived(dq_chip.at[0], 10)
+    arrived(dv_chip.at[0], 12)
+    for copy in stays:
+        copy.wait()
     for ref, which in (
         (key_out.at[0], 0), (key_out.at[0], 1), (key_out.at[0], 2), (query_out.at[0], 3), (value_out.at[0], 4),
         (value_out.at[0], 5), (value_out.at[0], 6), (sums_in, 7), (dk_out.at[0], 8), (dk_out.at[0], 9),
         (dq_chip.at[0], 10), (dk_chip.at[0], 11), (dv_chip.at[0], 12),
     ):
         wait_bytes(ref, near_send.at[which])
-    wait_bytes(tp.at[pl.ds(0, PLANE - 1), pl.ds(0, T_ROWS)], send.at[0])
+    wait_bytes(tp.at[pl.ds(0, PLANE - 1), pl.ds(0, ROWS)], send.at[0])
     wait_bytes(zb.at[pl.ds(0, NZ - 1)], send.at[2])
-    wait_bytes(tz.at[pl.ds(0, NZ - 1), pl.ds(0, T_ROWS)], send.at[3])
+    wait_bytes(tz.at[pl.ds(0, NZ - 1), pl.ds(0, ROWS)], send.at[3])
     wait_bytes(pb.at[pl.ds(0, PLANE - 1)], send.at[4])
     t_pair.wait_send()
     wait_bytes(ep.at[pl.ds(0, PLANE - 1), pl.ds(0, ROWS)], send.at[6])
     wait_bytes(ez.at[pl.ds(0, NZ - 1), pl.ds(0, ROWS)], send.at[7])
 
 
+def finish_kernel(loss_in, emb_in, dq_in, dk_in, dv_in, loss_out, emb_out, dq_out, dk_out, dv_out, sem):
+    pairs = ((dq_in, dq_out), (dk_in, dk_out), (dv_in, dv_out), (emb_in, emb_out))
+    copies = [pltpu.make_async_copy(source, goal, sem.at[i]) for i, (source, goal) in enumerate(pairs)]
+    for copy in copies:
+        copy.start()
+    loss_out[...] = loss_in[:, :1]
+    for copy in copies:
+        copy.wait()
+
+
+def finish(loss, *arrays):
+    vmem = pl.BlockSpec(memory_space=pltpu.VMEM)
+    shapes = [jax.ShapeDtypeStruct((1, 1), jnp.float32)] + [jax.ShapeDtypeStruct(x.shape, x.dtype) for x in arrays]
+    return pl.pallas_call(
+        finish_kernel,
+        name="finish",
+        out_shape=tuple(shapes),
+        in_specs=[vmem] * 5,
+        out_specs=(vmem,) + (pl.BlockSpec(memory_space=pl.ANY),) * 4,
+        scratch_shapes=[pltpu.SemaphoreType.DMA((4,))],
+        compiler_params=pltpu.CompilerParams(vmem_limit_bytes=4 * 1024 * 1024),
+    )(loss, *arrays)
+
+
 def shards(query_states, key_states, value_states, lengths, queue_keys, write_pos, teacher):
     vmem = pl.BlockSpec(memory_space=pltpu.VMEM)
-    smem = pl.BlockSpec(memory_space=pltpu.SMEM)
+    in_hbm = pl.BlockSpec(memory_space=pltpu.HBM)
     anywhere = pl.BlockSpec(memory_space=pl.ANY)
 
     def f32(*shape):
@@ -541,19 +577,25 @@
     def b16(*shape):
         return pltpu.VMEM(shape, jnp.bfloat16)
 
-    loss, unit_vec, grad_query, grad_key, grad_value = pl.pallas_call(
+    held = [
+        pltpu.with_memory_space_constraint(x, pltpu.HBM)
+        for x in (write_pos, query_states, key_states, value_states, queue_keys, teacher)
+    ]
+    results = pl.pallas_call(
         whole_kernel,
         name="whole",
         out_shape=(
-            jax.ShapeDtypeStruct((1, 1), jnp.float32),
-            jax.ShapeDtypeStruct((1, HEADS * HD), jnp.float32),
-            jax.ShapeDtypeStruct(query_states.shape, jnp.bfloat16),
-            jax.ShapeDtypeStruct(key_states.shape, jnp.bfloat16),
-            jax.ShapeDtypeStruct(value_states.shape, jnp.bfloat16),
+            pltpu.VMEM((1, 128), jnp.float32),
+            pltpu.VMEM((1, HEADS * HD), jnp.float32),
+            pltpu.VMEM(query_states.shape, jnp.bfloat16),
+            pltpu.VMEM(key_states.shape, jnp.bfloat16),
+            pltpu.VMEM(value_states.shape, jnp.bfloat16),
         ),
-        in_specs=[smem, smem] + [anywhere] * 5,
-        out_specs=(vmem,) * 5,
+        in_specs=[in_hbm, anywhere] + [in_hbm] * 5,
+        out_specs=(vmem, vmem, anywhere, vmem, anywhere),
         scratch_shapes=[
+            pltpu.SMEM((DOCS,), jnp.int32),
+            pltpu.SMEM((1,), jnp.int32),
             b16(2, BLOCK, WIDE),
             b16(2, BLOCK, KV),
             b16(2, BLOCK, KV),
@@ -570,10 +612,8 @@
             f32(2, BLOCK, KV),
             f32(2, BLOCK, KV),
             b16(2, BLOCK, KV),
-            b16(2, BLOCK, KV),
             b16(2, BLOCK, WIDE),
-            b16(2, BLOCK, WIDE),
-            b16(EXT, 2048),
+            b16(ENTRIES, 2048),
             f32(16, 128),
             f32(NZ, HALF, 128),
             f32(PLANE, HALF, 128),
@@ -592,16 +632,17 @@
             f32(DOCS, HEADS, 128),
             f32(16, 128),
             pltpu.SemaphoreType.REGULAR((3,)),
-            pltpu.SemaphoreType.DMA((11,)),
+            pltpu.SemaphoreType.DMA((13,)),
             pltpu.SemaphoreType.DMA((8,)),
             pltpu.SemaphoreType.DMA((8,)),
             pltpu.SemaphoreType.DMA((13,)),
             pltpu.SemaphoreType.DMA((13,)),
         ],
         compiler_params=pltpu.CompilerParams(
-            collective_id=0, has_side_effects=True, vmem_limit_bytes=56 * 1024 * 1024
+            collective_id=0, has_side_effects=True, vmem_limit_bytes=40 * 1024 * 1024
         ),
-    )(write_pos, lengths, query_states, key_states, value_states, queue_keys, teacher)
+    )(held[0], lengths, *held[1:])
+    loss, unit_vec, grad_query, grad_key, grad_value = finish(*results)
     return loss[0, 0], unit_vec, grad_query, grad_key, grad_value
 
 

time: 66.4 us -> 59.5 us (0.90)
  local copies, waits for them, and re-layouts: 4.18 us -> 0 us
  between operations: 3.06 us -> 1.29 us
  Pallas kernels: 58.9 us -> 58.1 us
    unnamed x10 -> x0, local copies, waits for them, and re-layouts: 4.18 us -> none
    pallas_call x1 -> x2, Pallas kernels: 58.9 us -> 58.1 us  [the longest x1 56.6 us: shards(): pl.pallas_call(whole_kernel, name='whole', out_shape=(pltpu.VMEM((1, 128)...]
where the time goes in v4:
time: 59.5 us; the launch traced here: 59.3 us
  Pallas kernels  58.1 us (98%)
  between operations  1.29 us (2%)
    pallas_call x1, Pallas kernels, shards(): pl.pallas_call(whole_kernel, name='whole', out_shape=(pltpu.VMEM((1, 128)...  56.6 us
    pallas_call x1, Pallas kernels, finish(): pl.pallas_call(finish_kernel, name='finish', out_shape=tuple(shapes), in_...  1.42 us

profile of v4, /device:TPU:1, one launch (start us, length us, event | category | flops | bytes accessed | tf_op | source)
XLA Modules:
  0.0 59.3 jit_solution(13938644188402970208)
XLA Ops:
  1.3 56.6 %whole.1 = (f32[1,128]{1,0:T(1,128)S(1)}, f32[1,2048]{1,0:T(1,128)S(1)}, bf16[1,128,2048]{2,1,0:T(8,128)(2,1)S(1)}, bf16[1,128,512]{2,1,0:T(8,128)(2,1)S(1)}, bf16[1,128,512]{2,1,0:T(8,128)(2,1)S(1)}) custom-call(s32[8]{0:T(128)} %pos_hbm.1, s32[1]{0:T(128)S(6)} %copy.12.len_hbm, bf16[1,128,2048]{2,1,0:T(8,128)(2,1)} %query_hbm.1, ...), custom_call_target="tpu_custom_call" | custom-call | tf_op jit(solution)/shard_map/whole/pallas_call | solution.py:584
  57.9 1.4 %finish.1 = (f32[1,1]{1,0:T(1,128)}, f32[1,2048]{1,0:T(1,128)}, bf16[1,128,2048]{2,1,0:T(8,128)(2,1)}, bf16[1,128,512]{2,1,0:T(8,128)(2,1)}, bf16[1,128,512]{2,1,0:T(8,128)(2,1)}) custom-call(f32[1,128]{1,0:T(1,128)S(1)} %get-tuple-element.15.loss_in, f32[1,2048]{1,0:T(1,128)S(1)} %get-tuple-element.16.emb_in, ...), custom_call_target="tpu_custom_call" | custom-call | tf_op jit(solution)/shard_map/finish/pallas_call | solution.py:558

commit v5 on v4

--- a/solution.py
+++ b/solution.py
@@ -114,7 +114,7 @@
 def whole_kernel(
     pos_hbm, len_hbm, query_hbm, key_hbm, value_hbm, queue_ref, teacher_hbm,
     loss_ref, emb_ref, dq_ref, dk_ref, dv_ref,
-    pos_ref, len_ref, query_out, key_out, value_out, query, keys, values, teacher_ref, prob, sums, sums_in, score,
+    pos_ref, len_ref, query, keys, values, teacher_ref, prob, sums, sums_in, score,
     dk_out, dk_in, dk_chip, dk_part, dv_chip, dq_chip,
     eff, mix, zb, pb, t_out, tp, tz, t_own, t_half, s_out, ep, ez, half_sum, ring_out,
     t_ring_out, t_full, unit_rows, e_ring_out,
@@ -139,12 +139,6 @@
 
     loads = []
     for i, (source, goal) in enumerate((
-        (key_hbm.at[0, :, pl.ds(0, KV)], key_out.at[0]),
-        (key_hbm.at[0, :, pl.ds(KV, KV)], key_out.at[1]),
-        (query_hbm.at[0, :, pl.ds(0, WIDE)], query_out.at[0]),
-        (query_hbm.at[0, :, pl.ds(WIDE, WIDE)], query_out.at[1]),
-        (value_hbm.at[0, :, pl.ds(0, KV)], value_out.at[0]),
-        (value_hbm.at[0, :, pl.ds(KV, KV)], value_out.at[1]),
         (teacher_hbm, teacher_ref),
         (queue_ref, eff),
         (key_hbm.at[0, :, pl.ds(pl.multiple_of(core * KV, KV), KV)], keys.at[2 + core]),
@@ -156,8 +150,6 @@
         loads.append(pltpu.make_async_copy(source, goal, load_sem.at[i]))
         loads[-1].start()
 
-    for i in range(6):
-        loads[i].wait()
     pl.semaphore_wait(barrier, len(first))
 
     def start(source, goal, which, to):
@@ -175,7 +167,7 @@
     def to_next(source, goal, which):
         for half in range(2):
             pltpu.make_async_remote_copy(
-                src_ref=source.at[half],
+                src_ref=source.at[0, :, pl.ds(half * KV, KV)],
                 dst_ref=goal.at[core],
                 send_sem=near_send.at[which + half],
                 recv_sem=near_recv.at[which + core],
@@ -183,11 +175,13 @@
                 device_id_type=MESH,
             ).start()
 
-    to_next(key_out, keys, 0)
-    start(key_out.at[1 - core], keys.at[2 + core], 2, twin)
-    start(query_out.at[1 - core], query.at[core], 3, twin)
-    start(value_out.at[1 - core], values.at[2 + core], 6, twin)
-    to_next(value_out, values, 4)
+    other_kv = pl.ds(pl.multiple_of((1 - core) * KV, KV), KV)
+    other_wide = pl.ds(pl.multiple_of((1 - core) * WIDE, WIDE), WIDE)
+    to_next(key_hbm, keys, 0)
+    start(key_hbm.at[0, :, other_kv], keys.at[2 + core], 2, twin)
+    start(query_hbm.at[0, :, other_wide], query.at[core], 3, twin)
+    start(value_hbm.at[0, :, other_kv], values.at[2 + core], 6, twin)
+    to_next(value_hbm, values, 4)
     for to in (shifted(dz=2), shifted(dz=NZ - 2), shifted(dx=2), shifted(dy=2), twin):
         pl.semaphore_signal(ready.at[0], inc=1, device_id=to, device_id_type=MESH)
 
@@ -195,9 +189,9 @@
     entry = lax.broadcasted_iota(jnp.int32, (DOCS, ENTRIES), 1) + base
     lane = lax.broadcasted_iota(jnp.int32, (DOCS, 128), 1)
     row = lax.broadcasted_iota(jnp.int32, (DOCS, 128), 0)
+    loads[0].wait()
+    loads[5].wait()
     loads[6].wait()
-    loads[11].wait()
-    loads[12].wait()
     teacher = teacher_ref[...]
     kept = jnp.ones((DOCS, ENTRIES), jnp.float32)
     there = jnp.zeros((DOCS, 128), jnp.float32)
@@ -217,7 +211,7 @@
         for h in range(HEADS):
             out[:, h // HALF, h % HALF] = part[:, h * HD : (h + 1) * HD]
 
-    loads[7].wait()
+    loads[1].wait()
     mixed = jnp.dot(two_halves(target), eff[...], preferred_element_type=jnp.float32)
     spread(t_out, mixed[:DOCS] + mixed[DOCS:])
     for c in range(2):
@@ -253,15 +247,15 @@
     def arrived(ref, which):
         wait_bytes(ref, near_recv.at[which])
 
-    for i in (8, 9, 10):
+    for i in (2, 3, 4):
         loads[i].wait()
-    arrived(key_out.at[0], 2)
-    arrived(query_out.at[0], 3)
+    arrived(keys.at[0], 2)
+    arrived(query.at[0], 3)
     weigh(0, 2)
     weigh(1, 1)
     weigh(1, 2)
-    arrived(key_out.at[0], 0)
-    arrived(key_out.at[0], 1)
+    arrived(keys.at[0], 0)
+    arrived(keys.at[0], 1)
     weigh(0, 0)
     weigh(0, 1)
     weigh(1, 0)
@@ -297,14 +291,13 @@
     )
     tp[mine] = t_out[grp, core]
 
-    arrived(value_out.at[0], 6)
-    arrived(sums_in, 7)
     length_float = length.astype(jnp.float32)
-    sums_all = sums[pl.ds(2, 2)] + sums_in[...]
+    for which in (6, 4, 5):
+        arrived(values.at[0], which)
     for g in range(GROUPS):
-        both = jnp.concatenate([sums_all[b, 4 * g : 4 * g + 4] for b in range(2)], 1)
+        both = jnp.concatenate([sums[b, 4 * g : 4 * g + 4] for b in range(4)], 1)
         split = jnp.concatenate([both, jnp.zeros_like(both)], 0)
-        tile = values[pl.ds(2, 2), :, g * HD : (g + 1) * HD].reshape(2 * BLOCK, HD)
+        tile = values[:, :, g * HD : (g + 1) * HD].reshape(4 * BLOCK, HD)
         out = jnp.dot(two_halves(split), tile, preferred_element_type=jnp.float32)
         half_sum[4 * g : 4 * g + 4] = (out[:4] + out[8:12]) / length_float
 
@@ -412,8 +405,8 @@
     mine_only = lax.broadcasted_iota(jnp.int32, (HALF, KV), 1) // HD == (
         lax.broadcasted_iota(jnp.int32, (HALF, KV), 0) // 4
     )
-    arrived(value_out.at[0], 4)
-    arrived(value_out.at[0], 5)
+    arrived(sums_in, 7)
+    sums_all = sums[pl.ds(2, 2)] + sums_in[...]
 
     wait_bytes(ep.at[pl.ds(0, PLANE - 1), pl.ds(0, ROWS)], recv.at[6])
     e_ring_out[...] = sum_slots(ep, PLANE)
@@ -436,12 +429,12 @@
         cot_diag, values[...].reshape(4 * BLOCK, KV), (((1,), (1,)), ((), ())), preferred_element_type=jnp.float32
     )
 
-    def scored(r):
-        for h in range(HALF):
+    def scored(r, g):
+        for h in range(4 * g, 4 * g + 4):
             part = prob[r, h]
             push = part * prob_grad[h : h + 1, r * BLOCK : (r + 3) * BLOCK]
             total = push[:, :BLOCK] + push[:, BLOCK : 2 * BLOCK] + push[:, 2 * BLOCK :]
-            score[r, h // 4, (h % 4) * BLOCK : (h % 4 + 1) * BLOCK] = (
+            score[r, g, (h % 4) * BLOCK : (h % 4 + 1) * BLOCK] = (
                 push - part * jnp.sum(total, 1, keepdims=True)
             ).astype(jnp.bfloat16)
 
@@ -459,12 +452,11 @@
                 total = one if total is None else total + one
         return total * HD ** (-0.5)
 
-    def send_back(block):
-        for g in range(GROUPS):
-            dk_out[block, :, g * HD : (g + 1) * HD] = key_grad(block, g).astype(jnp.bfloat16)
+    def send_back(block, g):
+        dk_out[block, g] = key_grad(block, g).astype(jnp.bfloat16)
         pltpu.make_async_remote_copy(
-            src_ref=dk_out.at[block],
-            dst_ref=dk_in.at[core],
+            src_ref=dk_out.at[block, g],
+            dst_ref=dk_in.at[core, g],
             send_sem=near_send.at[8 + block],
             recv_sem=near_recv.at[8 + core],
             device_id=beside(-1, block),
@@ -479,10 +471,10 @@
                 h = 4 * g + j
                 dq_chip[r, :, h * HD : (h + 1) * HD] = dq[j * BLOCK : (j + 1) * BLOCK].astype(jnp.bfloat16)
 
-    scored(0)
-    send_back(0)
-    scored(1)
-    send_back(1)
+    for r in range(2):
+        for g in range(GROUPS):
+            scored(r, g)
+            send_back(r, g)
     own_wide = pl.ds(pl.multiple_of(core * WIDE, WIDE), WIDE)
     own_kv = pl.ds(pl.multiple_of(core * KV, KV), KV)
     query_grad(1 - core)
@@ -519,17 +511,16 @@
     arrived(dk_chip.at[0], 11)
     for half in range(2):
         arrived(dk_out.at[0], 8 + half)
-        dk_ref[0, :, half * KV : (half + 1) * KV] = (dk_part[half] + dk_in[half].astype(jnp.float32)).astype(
-            jnp.bfloat16
-        )
+        arrived_part = jnp.concatenate([dk_in[half, g] for g in range(GROUPS)], 1).astype(jnp.float32)
+        dk_ref[0, :, half * KV : (half + 1) * KV] = (dk_part[half] + arrived_part).astype(jnp.bfloat16)
 
     arrived(dq_chip.at[0], 10)
     arrived(dv_chip.at[0], 12)
     for copy in stays:
         copy.wait()
     for ref, which in (
-        (key_out.at[0], 0), (key_out.at[0], 1), (key_out.at[0], 2), (query_out.at[0], 3), (value_out.at[0], 4),
-        (value_out.at[0], 5), (value_out.at[0], 6), (sums_in, 7), (dk_out.at[0], 8), (dk_out.at[0], 9),
+        (keys.at[0], 0), (keys.at[0], 1), (keys.at[0], 2), (query.at[0], 3), (values.at[0], 4),
+        (values.at[0], 5), (values.at[0], 6), (sums_in, 7), (dk_out.at[0], 8), (dk_out.at[0], 9),
         (dq_chip.at[0], 10), (dk_chip.at[0], 11), (dv_chip.at[0], 12),
     ):
         wait_bytes(ref, near_send.at[which])
@@ -597,9 +588,6 @@
             pltpu.SMEM((DOCS,), jnp.int32),
             pltpu.SMEM((1,), jnp.int32),
             b16(2, BLOCK, WIDE),
-            b16(2, BLOCK, KV),
-            b16(2, BLOCK, KV),
-            b16(2, BLOCK, WIDE),
             b16(4, BLOCK, KV),
             b16(4, BLOCK, KV),
             f32(DOCS, ENTRIES),
@@ -607,8 +595,8 @@
             f32(4, HALF, BLOCK),
             f32(2, HALF, BLOCK),
             b16(2, GROUPS, 4 * BLOCK, 3 * BLOCK),
-            b16(2, BLOCK, KV),
-            b16(2, BLOCK, KV),
+            b16(2, GROUPS, BLOCK, HD),
+            b16(2, GROUPS, BLOCK, HD),
             f32(2, BLOCK, KV),
             f32(2, BLOCK, KV),
             b16(2, BLOCK, KV),
@@ -632,7 +620,7 @@
             f32(DOCS, HEADS, 128),
             f32(16, 128),
             pltpu.SemaphoreType.REGULAR((3,)),
-            pltpu.SemaphoreType.DMA((13,)),
+            pltpu.SemaphoreType.DMA((7,)),
             pltpu.SemaphoreType.DMA((8,)),
             pltpu.SemaphoreType.DMA((8,)),
             pltpu.SemaphoreType.DMA((13,)),

time: 59.5 us -> 56.7 us (0.953)
  Pallas kernels: 58.1 us -> 55.3 us
    pallas_call x1, Pallas kernels: 56.6 us -> 53.9 us  [shards(): pl.pallas_call(whole_kernel, name='whole', out_shape=(pltpu.VMEM((1, 128)...]
where the time goes in v5:
time: 56.7 us; the launch traced here: 56.6 us
  Pallas kernels  55.3 us (98%)
  between operations  1.29 us (2%)
    pallas_call x1, Pallas kernels, shards(): pl.pallas_call(whole_kernel, name='whole', out_shape=(pltpu.VMEM((1, 128)...  53.9 us
    pallas_call x1, Pallas kernels, finish(): pl.pallas_call(finish_kernel, name='finish', out_shape=tuple(shapes), in_...  1.42 us

profile of v5, /device:TPU:1, one launch (start us, length us, event | category | flops | bytes accessed | tf_op | source)
XLA Modules:
  0.0 56.6 jit_solution(15995510434861051764)
XLA Ops:
  1.3 53.9 %whole.1 = (f32[1,128]{1,0:T(1,128)S(1)}, f32[1,2048]{1,0:T(1,128)S(1)}, bf16[1,128,2048]{2,1,0:T(8,128)(2,1)S(1)}, bf16[1,128,512]{2,1,0:T(8,128)(2,1)S(1)}, bf16[1,128,512]{2,1,0:T(8,128)(2,1)S(1)}) custom-call(s32[8]{0:T(128)} %pos_hbm.1, s32[1]{0:T(128)S(6)} %copy.12.len_hbm, bf16[1,128,2048]{2,1,0:T(8,128)(2,1)} %query_hbm.1, ...), custom_call_target="tpu_custom_call" | custom-call | tf_op jit(solution)/shard_map/whole/pallas_call | solution.py:575
  55.2 1.4 %finish.1 = (f32[1,1]{1,0:T(1,128)}, f32[1,2048]{1,0:T(1,128)}, bf16[1,128,2048]{2,1,0:T(8,128)(2,1)}, bf16[1,128,512]{2,1,0:T(8,128)(2,1)}, bf16[1,128,512]{2,1,0:T(8,128)(2,1)}) custom-call(f32[1,128]{1,0:T(1,128)S(1)} %get-tuple-element.15.loss_in, f32[1,2048]{1,0:T(1,128)S(1)} %get-tuple-element.16.emb_in, ...), custom_call_target="tpu_custom_call" | custom-call | tf_op jit(solution)/shard_map/finish/pallas_call | solution.py:549

commit v6 on v5

--- a/solution.py
+++ b/solution.py
@@ -63,7 +63,7 @@
     x_hi, z, core, grp = position()
     mine = x_hi * 16 + core * 8 + grp
 
-    def one(k, carry):
+    def one(k):
         px, pc, pg = plane_peer(31 - k)
         pltpu.make_async_remote_copy(
             src_ref=src_of(pc, pg),
@@ -73,15 +73,15 @@
             device_id=device(px, z, pc, pg),
             device_id_type=MESH,
         ).start()
-        return carry
-
-    lax.fori_loop(0, PLANE - 1, one, 0)
+
+    for k in range(PLANE - 1):
+        one(k)
 
 
 def send_ring(src, dst, send_sem, recv_sem):
     x_hi, z, core, grp = position()
 
-    def one(k, carry):
+    def one(k):
         pltpu.make_async_remote_copy(
             src_ref=src,
             dst_ref=dst(z),
@@ -90,9 +90,9 @@
             device_id=device(x_hi, (z + z_offset(k)) % NZ, core, grp),
             device_id_type=MESH,
         ).start()
-        return carry
-
-    lax.fori_loop(0, NZ - 1, one, 0)
+
+    for k in range(NZ - 1):
+        one(k)
 
 
 def wait_bytes(ref, sem):
@@ -533,12 +533,12 @@
     wait_bytes(ez.at[pl.ds(0, NZ - 1), pl.ds(0, ROWS)], send.at[7])
 
 
-def finish_kernel(loss_in, emb_in, dq_in, dk_in, dv_in, loss_out, emb_out, dq_out, dk_out, dv_out, sem):
-    pairs = ((dq_in, dq_out), (dk_in, dk_out), (dv_in, dv_out), (emb_in, emb_out))
+def finish_kernel(loss_in, emb_in, dq_in, dk_in, dv_in, loss_out, emb_out, dq_out, dk_out, dv_out, loss_here, sem):
+    pairs = ((dq_in, dq_out), (dk_in, dk_out), (dv_in, dv_out), (emb_in, emb_out), (loss_here, loss_out))
+    loss_here[...] = loss_in[:, :1]
     copies = [pltpu.make_async_copy(source, goal, sem.at[i]) for i, (source, goal) in enumerate(pairs)]
     for copy in copies:
         copy.start()
-    loss_out[...] = loss_in[:, :1]
     for copy in copies:
         copy.wait()
 
@@ -551,8 +551,8 @@
         name="finish",
         out_shape=tuple(shapes),
         in_specs=[vmem] * 5,
-        out_specs=(vmem,) + (pl.BlockSpec(memory_space=pl.ANY),) * 4,
-        scratch_shapes=[pltpu.SemaphoreType.DMA((4,))],
+        out_specs=(pl.BlockSpec(memory_space=pl.ANY),) * 5,
+        scratch_shapes=[pltpu.VMEM((1, 1), jnp.float32), pltpu.SemaphoreType.DMA((5,))],
         compiler_params=pltpu.CompilerParams(vmem_limit_bytes=4 * 1024 * 1024),
     )(loss, *arrays)
 

time: 56.7 us -> 55.7 us (0.982)
  Pallas kernels: 55.3 us -> 54.3 us
where the time goes in v6:
time: 55.7 us; the launch traced here: 55.6 us
  Pallas kernels  54.3 us (97%)
  between operations  1.29 us (2%)
    pallas_call x1, Pallas kernels, shards(): pl.pallas_call(whole_kernel, name='whole', out_shape=(pltpu.VMEM((1, 128)...  53.4 us

profile of v6, /device:TPU:1, one launch (start us, length us, event | category | flops | bytes accessed | tf_op | source)
XLA Modules:
  0.0 55.6 jit_solution(5255929361846869186)
XLA Ops:
  1.3 53.4 %whole.1 = (f32[1,128]{1,0:T(1,128)S(1)}, f32[1,2048]{1,0:T(1,128)S(1)}, bf16[1,128,2048]{2,1,0:T(8,128)(2,1)S(1)}, bf16[1,128,512]{2,1,0:T(8,128)(2,1)S(1)}, bf16[1,128,512]{2,1,0:T(8,128)(2,1)S(1)}) custom-call(s32[8]{0:T(128)} %pos_hbm.1, s32[1]{0:T(128)S(6)} %copy.12.len_hbm, bf16[1,128,2048]{2,1,0:T(8,128)(2,1)} %query_hbm.1, ...), custom_call_target="tpu_custom_call" | custom-call | tf_op jit(solution)/shard_map/whole/pallas_call | solution.py:575
  54.7 0.9 %finish.1 = (f32[1,1]{1,0:T(1,128)}, f32[1,2048]{1,0:T(1,128)}, bf16[1,128,2048]{2,1,0:T(8,128)(2,1)}, bf16[1,128,512]{2,1,0:T(8,128)(2,1)}, bf16[1,128,512]{2,1,0:T(8,128)(2,1)}) custom-call(f32[1,128]{1,0:T(1,128)S(1)} %get-tuple-element.15.loss_in, f32[1,2048]{1,0:T(1,128)S(1)} %get-tuple-element.16.emb_in, ...), custom_call_target="tpu_custom_call" | custom-call | tf_op jit(solution)/shard_map/finish/pallas_call | solution.py:549
